TPU v7x, 512 devices: a whole 4x4x16 slice. The times are simulated.
512 devices in a mesh: rows: 128 (over z, x_lo, y), batch: 4 (over x_hi, core).
Axes of the slice: x: 4 (x_hi: 2, x_lo: 2; x = x_hi * 2 + x_lo), y: 4, z: 16, core: 2. Of those that a mesh axis runs over, the one named last changes fastest.
Arguments:
- hidden_states: bfloat16 [16384, 1280], P(('batch', 'rows')), parts along dimension 0, may hold values from -1000 to 1000
- norm_gain: float32 [1280], replicated, may hold values from 0.1 to 1.9
- norm_bias: float32 [1280], replicated, may hold values from -3 to 3
- query_weight: bfloat16 [1280, 640], replicated, may hold values from -0.15625 to 0.15625
- key_weight: bfloat16 [1280, 640], replicated, may hold values from -0.15625 to 0.15625
- value_weight: bfloat16 [1280, 640], replicated, may hold values from -0.15625 to 0.15625
- stale_keys: bfloat16 [16384, 640], P(('batch', 'rows')), parts along dimension 0, may hold values from -370 to 370
- stale_values: bfloat16 [16384, 640], P(('batch', 'rows')), parts along dimension 0, may hold values from -6 to 6
Outputs:
- attention: bfloat16 [16384, 640], P(('batch', 'rows')), parts along dimension 0
- fresh_keys: bfloat16 [16384, 640], P(('batch', 'rows')), parts along dimension 0
- fresh_values: bfloat16 [16384, 640], P(('batch', 'rows')), parts along dimension 0
There are 4 independent parts, one for each index of `batch`. A program takes and returns all parts, laid end to end along the dimension named above; an argument that names none is the same for every part. Nothing has to cross between parts.
All inputs are finite; a program needn't handle non-finite values.
Results may differ from a plain program's by a relative error of at most 0.013.
The roundings to bfloat16 on the way count: a program that leaves them out, or rounds other values in their place, can miss the bound.
Values may be sent and summed in bfloat16 or wider, within the bound.
A program may use at most 64 MiB of HBM per device.

v0:
```python
import jax
import jax.numpy as jnp
from jax import lax
from jax.sharding import PartitionSpec as P

CHANNELS = 1280
GROUPS = 32
HEADS = 10
HEAD_DIM = 64


EPSILON = 1e-05


def group_average(channel_totals, count):
    grouped = channel_totals.reshape(GROUPS, -1).sum(axis=1) / count
    return jnp.repeat(grouped, channel_totals.shape[0] // GROUPS)


def head_scores(query, key_rows):
    keys_three = key_rows.reshape(key_rows.shape[0], key_rows.shape[1] // HEAD_DIM, HEAD_DIM)
    scaling = HEAD_DIM ** (-0.5)
    return (
        jnp.einsum("qhd,khd->qhk", query, keys_three, preferred_element_type=jnp.float32) * scaling
    )


def head_values(exps, value_rows):
    values_three = value_rows.reshape(
        value_rows.shape[0], value_rows.shape[1] // HEAD_DIM, HEAD_DIM
    )
    return jnp.einsum(
        "qhk,khd->qhd", exps.astype(jnp.bfloat16), values_three, preferred_element_type=jnp.float32
    )


def plain_attend(query, key_rows, value_rows):
    scores = head_scores(query, key_rows)
    largest = jnp.max(scores, axis=-1)
    exps = jnp.exp(scores - largest[..., None])
    totals = jnp.sum(exps, axis=-1)
    weighted = head_values(exps, value_rows)
    return weighted / totals[..., None]


def on_device(
    hidden_states,
    norm_gain,
    norm_bias,
    query_weight,
    key_weight,
    value_weight,
    stale_keys,
    stale_values,
):
    local_rows = hidden_states.shape[0]
    total_rows = local_rows * lax.axis_size("rows")
    group_count = total_rows * (CHANNELS // GROUPS)
    widened = hidden_states.astype(jnp.float32)
    sums = lax.psum(jnp.sum(widened, axis=0), "rows")
    mean_chan = group_average(sums, group_count)
    centered = widened - mean_chan
    squares = lax.psum(jnp.sum(centered * centered, axis=0), "rows")
    var_chan = group_average(squares, group_count)
    normed = ((widened - mean_chan) * lax.rsqrt(var_chan + EPSILON) * norm_gain + norm_bias).astype(
        jnp.bfloat16
    )
    query_flat = jnp.dot(normed, query_weight, preferred_element_type=jnp.float32).astype(
        jnp.bfloat16
    )
    query = query_flat.reshape(local_rows, HEADS, HEAD_DIM)
    fresh_keys = jnp.dot(normed, key_weight, preferred_element_type=jnp.float32).astype(
        jnp.bfloat16
    )
    fresh_values = jnp.dot(normed, value_weight, preferred_element_type=jnp.float32).astype(
        jnp.bfloat16
    )
    own_start = lax.axis_index("rows") * local_rows
    key_all, value_all = (
        lax.all_gather(stale_keys, "rows", axis=0, tiled=True),
        lax.all_gather(stale_values, "rows", axis=0, tiled=True),
    )
    key_all = lax.dynamic_update_slice(key_all, fresh_keys, (own_start, 0))
    value_all = lax.dynamic_update_slice(value_all, fresh_values, (own_start, 0))
    attention = plain_attend(query, key_all, value_all).reshape(local_rows, -1).astype(jnp.bfloat16)
    return (attention, fresh_keys, fresh_values)


def solution(mesh):
    placed = (
        P(("batch", "rows"), None),
        P(),
        P(),
        P(),
        P(),
        P(),
        P(("batch", "rows"), None),
        P(("batch", "rows"), None),
    )
    return jax.shard_map(
        on_device,
        mesh=mesh,
        in_specs=placed,
        out_specs=(
            P(("batch", "rows"), None),
            P(("batch", "rows"), None),
            P(("batch", "rows"), None),
        ),
        check_vma=False,
    )
```

profile of v0, /device:TPU:6, one launch (start us, length us, event | category | flops | bytes accessed | tf_op | source)
XLA Modules:
  0.0 1272.8 jit_solution(7467857796500288936)
XLA Ops:
  7.2 0.0 copy-start
  7.2 0.0 all-gather.5.cloned.1.call-start
  7.2 0.7 all-gather.5.cloned.1.call-update
  7.9 0.0 all-gather.3.cloned.1.call-start
  8.0 0.7 all-gather.3.cloned.1.call-update
  8.7 0.9 convert_reduce_fusion
  9.6 0.1 reshape.38
  9.7 609.5 %psum.14 = f32[32,40]{1,0:T(8,128)S(1)} all-reduce(f32[32,40]{1,0:T(8,128)S(1)} %reshape.38), channel_id=1, replica_groups=mesh['rows'=128,'batch'=4] {'rows'}, use_global_device_ids=true, to_apply=%region_1.0 | all-reduce | flops 1280 | bytes 10240 | tf_op jit(solution)/shard_map/psum | solution.py:60
  619.1 0.1 reduce_sum.46
  619.2 0.1 broadcast_in_dim.4
  619.3 0.1 sub.10
  619.4 0.9 fusion.17
  620.3 0.1 reshape.39
  620.4 604.5 %psum.15 = f32[32,40]{1,0:T(8,128)S(1)} all-reduce(f32[32,40]{1,0:T(8,128)S(1)} %reshape.39), channel_id=1, replica_groups=mesh['rows'=128,'batch'=4] {'rows'}, use_global_device_ids=true, to_apply=%region_4.0 | all-reduce | flops 1280 | bytes 10240 | tf_op jit(solution)/shard_map/psum | solution.py:63
  1224.9 0.1 reduce_sum.48
  1225.0 0.1 broadcast_in_dim.5
  1225.1 0.1 rsqrt.12
  1225.2 0.0 copy-done
  1225.2 1.2 convolution_convert_fusion.1
  1226.4 0.0 copy-start.2
  1226.4 0.2 copy.29
  1226.6 1.9 convolution_convert_fusion
  1228.5 0.1 reshape.42
  1228.6 1.8 convolution_convert_fusion.2
  1230.5 0.0 copy-start.3
  1230.5 0.2 copy.27
  1230.7 0.0 all-gather.5.cloned.1.call-done
  1230.7 7.9 copy.28
  1238.6 0.0 copy-done.2
  1238.6 0.0 copy-done.3
  1238.6 3.2 dynamic_update_slice.7
  1241.8 3.5 fusion.25
  1245.3 0.0 copy-start.1
  1245.3 2.4 copy-done.1
  1247.6 0.8 fusion.1
  1248.4 0.0 all-gather.3.cloned.1.call-done
  1248.5 7.9 copy.26
  1256.3 3.2 dynamic_update_slice.6
  1259.5 5.6 fusion.12
  1265.2 0.8 convert_element_type.31
  (3 shorter events, 0.1 us)
Async XLA Ops:
  7.2 1218.0 %copy-start = (bf16[1280,640]{1,0:T(8,128)(2,1)S(1)}, bf16[1280,640]{1,0:T(8,128)(2,1)}, u32[]{:S(2)}) copy-start(bf16[1280,640]{1,0:T(8,128)(2,1)} %param.12) | copy-start | bytes 4915204
  7.2 1223.5 %all-gather.5.cloned.1.call-start = ((), (), s32[]{:S(2)}) async-start(), calls=%async_computation.1 | async-start | bytes 5283840 | tf_op jit(solution)/shard_map/all_gather | solution.py:80
  7.9 1240.5 %all-gather.3.cloned.1.call-start = ((), (), s32[]{:S(2)}) async-start(), calls=%async_computation | async-start | bytes 5283840 | tf_op jit(solution)/shard_map/all_gather | solution.py:81
  1226.4 12.2 copy-start.2
  1230.5 8.1 copy-start.3
  1245.3 2.4 copy-start.1
Sparse Core Ops, SparseCore 0:
  10.1 597.2 all-gather.4
  609.5 593.4 all-gather.2
where the time goes:
time: 1280 us; the launch traced here: 1270 us
  blocking collectives  1210 us (95%)
  local copies, waits for them, and re-layouts  26.3 us (2%)
  between operations  14.2 us (1%)
  matrix products  14.1 us (1%)
    psum x1, blocking collectives, on_device(): sums = lax.psum(jnp.sum(widened, axis=0), 'rows')  609 us
    psum x1, blocking collectives, on_device(): squares = lax.psum(jnp.sum(centered * centered, axis=0), 'rows')  604 us
  transfers between devices with their start and end apart: 2, of which 0 were waited for; matrix products, arithmetic and copies ran while one was open for 2% of the time, Pallas kernels for 0%

commit v1 on v0

v1 whole, which is shorter than its diff:
```python
import functools

import jax
import jax.numpy as jnp
from jax import lax
from jax.experimental import pallas as pl
from jax.experimental.pallas import tpu as pltpu
from jax.sharding import PartitionSpec as P

CHANNELS = 1280
GROUPS = 32
GROUP_WIDTH = CHANNELS // GROUPS
HEADS = 10
HEAD_DIM = 64
WIDTH = HEADS * HEAD_DIM
PAIRS = HEADS // 2
EPSILON = 1e-05
PLANE = 8

F32 = jnp.float32
BF16 = jnp.bfloat16
MESH = pl.DeviceIdType.MESH
NT = (((1,), (1,)), ((), ()))


def exact_dot(value, right, dims):
    first = value.astype(BF16).astype(F32)
    second = (value - first).astype(BF16).astype(F32)
    terms = jnp.concatenate([first, second, value - first - second], axis=0).astype(BF16)
    out = lax.dot_general(terms, right, dims, preferred_element_type=F32)
    return out[0:8] + out[8:16] + out[16:24]


def to_groups(value, member):
    return exact_dot(value, member, (((1,), (0,)), ((), ())))


def to_channels(value, member):
    return exact_dot(value, member, NT)


def kernel(
    depth, plane, tokens,
    x_in, gain, bias, wq_in, wk_in, wv_in, k_in, v_in,
    result,
    x_own, kbuf, vbuf, wq, wk, wv, member, qbuf, st1, st2,
    part_o, part_m, part_l, obuf, rbuf, ostat, ostat_packed, rstat_packed,
    in_sem, s1_send, s1_recv, s2_send, s2_recv, q_send, q_recv,
    k_send, k_recv, v_send, v_recv, o_send, o_recv, t_send, t_recv,
):
    row = lax.axis_index("rows")
    z, p = row // plane, lax.rem(row, plane)
    half = depth // 2

    def in_plane(step):
        return {"rows": z * plane + lax.rem(p + step, plane)}

    def in_depth(step):
        return {"rows": lax.rem(z + step, depth) * plane + p}

    def remote(src, dst, send, recv, device):
        return pltpu.make_async_remote_copy(
            src_ref=src, dst_ref=dst, send_sem=send, recv_sem=recv,
            device_id=device, device_id_type=MESH,
        )

    barrier = pltpu.get_barrier_semaphore()

    @pl.loop(1, depth)
    def _(step):
        pl.semaphore_signal(barrier, inc=1, device_id=in_depth(step), device_id_type=MESH)

    @pl.loop(1, plane)
    def _(step):
        pl.semaphore_signal(barrier, inc=1, device_id=in_plane(step), device_id_type=MESH)

    loads = [
        pltpu.make_async_copy(src, dst, in_sem.at[i])
        for i, (src, dst) in enumerate(
            [(x_in, x_own), (k_in, kbuf.at[0]), (v_in, vbuf.at[0]),
             (wq_in, wq), (wk_in, wk), (wv_in, wv)]
        )
    ]
    for load in loads:
        load.start()

    channel = lax.broadcasted_iota(jnp.int32, (CHANNELS, 128), 0)
    group = lax.broadcasted_iota(jnp.int32, (CHANNELS, 128), 1)
    first = group * GROUP_WIDTH
    inside = (channel >= first) & (channel < first + GROUP_WIDTH) & (group < GROUPS)
    member[...] = jnp.where(inside, 1.0, 0.0).astype(BF16)

    loads[0].wait()
    x = x_own[...]
    count = tokens * GROUP_WIDTH
    mean = jnp.sum(jnp.dot(x, member[...], preferred_element_type=F32), axis=0, keepdims=True) / count
    centered = x.astype(F32) - to_channels(jnp.broadcast_to(mean, (8, 128)), member[...])[0:1]
    squares = jnp.sum((centered * centered).reshape(tokens // 8, 8, CHANNELS), axis=0)
    var = jnp.sum(to_groups(squares, member[...]), axis=0, keepdims=True) / count
    st1[0, 0:1, :] = mean
    st1[0, 1:2, :] = var
    loads[1].wait()
    loads[2].wait()

    pl.semaphore_wait(barrier, plane + depth - 2)

    def stat1(step):
        return remote(st1.at[0], st1.at[step], s1_send.at[step], s1_recv.at[step], in_plane(step))

    def stat2(step):
        return remote(st2.at[0], st2.at[step], s2_send.at[step], s2_recv.at[step], in_depth(step))

    def share(pair, step):
        return remote(
            qbuf.at[pair, 0], qbuf.at[pair, step], q_send.at[pair, step], q_recv.at[pair, step],
            in_plane(step),
        )

    order = [0]
    for step in range(1, half):
        order += [step, depth - step]
    order += [half]
    middle = half
    place = {block: at if at < middle else at + 1 for at, block in enumerate(order)}

    def hop(buf, send, recv, way, step):
        if way == 0:
            ends, device = (step, step + 1), in_depth(1)
        else:
            ends, device = ((depth - step) % depth, depth - step - 1), in_depth(depth - 1)
        here, there = place[ends[0]], place[ends[1]]
        return remote(buf.at[here], buf.at[there], send.at[way, step], recv.at[there], device)

    chains = [
        (kbuf, k_send, k_recv, 0, half),
        (vbuf, v_send, v_recv, 1, half),
        (kbuf, k_send, k_recv, 1, half - 1),
        (vbuf, v_send, v_recv, 0, half - 1),
    ]

    def ring(step):
        for buf, send, recv, way, length in chains:
            if step <= length:
                if step > 0:
                    hop(buf, send, recv, way, step - 1).wait_recv()
                if step < length:
                    hop(buf, send, recv, way, step).start()

    def rings(first, last):
        for step in range(first, min(last, half) + 1):
            ring(step)

    def merged(stats):
        means, spread = stats[:, 0, :], stats[:, 1, :]
        mean = jnp.mean(means, axis=0, keepdims=True)
        apart = means - mean
        return mean, jnp.mean(spread + apart * apart, axis=0, keepdims=True)

    @pl.loop(1, plane)
    def _(step):
        stat1(step).start()

    rings(0, 0)

    @pl.loop(1, plane)
    def _(step):
        stat1(step).wait_recv()

    mean, var = merged(st1[...])
    st2[0, 0:1, :] = mean
    st2[0, 1:2, :] = var

    @pl.loop(1, depth)
    def _(step):
        stat2(step).start()

    rings(1, 1)

    @pl.loop(1, depth)
    def _(step):
        stat2(step).wait_recv()

    mean, var = merged(st2[...])
    line = lax.broadcasted_iota(jnp.int32, (8, 128), 0)
    wide = to_channels(jnp.where(line == 0, mean, lax.rsqrt(var + EPSILON)), member[...])
    mean_chan = wide[0:1]
    scale_chan = wide[1:2] * gain[...].reshape(1, CHANNELS)
    bias_chan = bias[...].reshape(1, CHANNELS)
    normed = ((x_own[...].astype(F32) - mean_chan) * scale_chan + bias_chan).astype(BF16)

    rings(2, 2)
    loads[3].wait()
    query = jnp.dot(normed, wq[...], preferred_element_type=F32).astype(BF16)
    query = query * jnp.asarray(HEAD_DIM**-0.5, BF16)
    for pair in range(PAIRS):
        qbuf[pair, 0] = query[:, pair * 128 : (pair + 1) * 128]

    @pl.loop(0, PAIRS)
    def _(pair):
        @pl.loop(1, plane)
        def _(step):
            share(pair, step).start()

    rings(3, 3)
    loads[4].wait()
    fresh = jnp.dot(normed, wk[...], preferred_element_type=F32).astype(BF16)
    kbuf[middle] = fresh
    result[1] = fresh
    rings(4, 4)
    loads[5].wait()
    fresh = jnp.dot(normed, wv[...], preferred_element_type=F32).astype(BF16)
    vbuf[middle] = fresh
    result[2] = fresh

    lane = lax.broadcasted_iota(jnp.int32, (1, 128), 1)
    low = lane < HEAD_DIM
    masks = (jnp.where(low, 1.0, 0.0).astype(BF16), jnp.where(low, 0.0, 1.0).astype(BF16))
    keys_len = half * tokens
    ones = jnp.ones((keys_len, 128), BF16)

    def attend(query, start, pair):
        cols = pl.ds(pl.multiple_of(pair * 128, 128), 128)
        keys = kbuf[start : start + half, :, cols].reshape(keys_len, 128)
        values = vbuf[start : start + half, :, cols].reshape(keys_len, 128)
        count = query.shape[0]
        both = jnp.concatenate([query * masks[0], query * masks[1]], axis=0)
        scores = lax.dot_general(both, keys, NT, preferred_element_type=F32)
        largest = jnp.max(scores, axis=-1, keepdims=True)
        exps = jnp.exp(scores - largest).astype(BF16)
        sums = jnp.dot(exps, jnp.concatenate([values, ones], axis=1), preferred_element_type=F32)

        def pick(tall):
            return jnp.where(low, tall[0:count], tall[count:])

        return pick(sums[:, 0:128]), pick(jnp.broadcast_to(largest, (2 * count, 128))), pick(sums[:, 128:])

    def keep(pair, first, last, parts):
        for buf, value in zip((part_o, part_m, part_l), parts):
            buf[pair, first:last] = value

    rows = plane * tokens

    @pl.loop(0, PAIRS)
    def _(pair):
        keep(pair, 0, tokens, attend(qbuf[pair, 0], 1, pair))

    rings(5, 6)

    def first_half(pair):
        @pl.loop(1, plane)
        def _(step):
            share(pair, step).wait_recv()

        others = qbuf[pair, 1:plane].reshape(rows - tokens, 128)
        keep(pair, tokens, rows, attend(others, 0, pair))

    pl.loop(0, 2)(first_half)
    rings(7, 7)
    pl.loop(2, PAIRS)(first_half)
    rings(8, half)

    def back(pair, slot):
        return remote(
            obuf.at[pair, slot], rbuf.at[pair, slot], o_send.at[pair, slot], o_recv.at[pair, slot],
            in_plane(plane - slot),
        )

    def stat_back(slot):
        return remote(
            ostat_packed.at[slot], rstat_packed.at[slot], t_send.at[slot], t_recv.at[slot],
            in_plane(plane - slot),
        )

    ostat[...] = jnp.zeros_like(ostat)
    within = lax.rem(lane, HEAD_DIM)

    @pl.loop(0, PAIRS)
    def _(pair):
        out, largest, total = attend(qbuf[pair].reshape(rows, 128), half + 1, pair)
        old_largest = part_m[pair]
        top = jnp.maximum(largest, old_largest)
        now, before = jnp.exp(largest - top), jnp.exp(old_largest - top)
        out = (out * now + part_o[pair] * before).astype(BF16)
        total = total * now + part_l[pair] * before
        obuf[pair] = out.reshape(plane, tokens, 128)

        @pl.loop(1, plane)
        def _(slot):
            back(pair, slot).start()

        stats = jnp.where(within == pair, top, ostat[...])
        ostat[...] = jnp.where(within == pair + 8, total, stats)

    packs = tokens // 8
    tiles = ostat[...].reshape(plane, packs, 8, 128)
    packed = sum(
        pltpu.roll(tiles[:, pack].reshape(plane * 8, 128), 16 * pack, 1) if pack else tiles[:, pack].reshape(plane * 8, 128)
        for pack in range(packs)
    )
    ostat_packed[...] = packed.reshape(plane, 8, 128)

    @pl.loop(1, plane)
    def _(slot):
        stat_back(slot).start()

    head_lane = lax.broadcasted_iota(jnp.int32, (128, WIDTH), 0)
    feature = lax.broadcasted_iota(jnp.int32, (128, WIDTH), 1)
    from_feature = lax.rem(head_lane, HEAD_DIM) * 128 + (head_lane // HEAD_DIM) * HEAD_DIM
    spread = jnp.where((feature >= from_feature) & (feature < from_feature + HEAD_DIM), 1.0, 0.0).astype(BF16)
    rstat_packed[0] = ostat_packed[0]

    @pl.loop(1, plane)
    def _(slot):
        stat_back(slot).wait_recv()

    packed = rstat_packed[...].reshape(plane * 8, 128)
    tiles = [pltpu.roll(packed, 128 - 16 * pack, 1) if pack else packed for pack in range(packs)]
    stats = jnp.concatenate([tile.reshape(plane, 8, 128) for tile in tiles], axis=1)
    largest = jnp.max(stats, axis=0, keepdims=True)
    used = within < PAIRS
    weights = jnp.where(used, jnp.exp(stats - largest), 0.0)
    sums = pltpu.roll(stats.reshape(rows, 128), 120, 1).reshape(plane, tokens, 128)
    totals = jnp.where(used, jnp.sum(weights * sums, axis=0, keepdims=True), 1.0)
    shares = (weights / totals).reshape(rows, 128)
    upper = shares.astype(BF16)
    lower = (shares - upper.astype(F32)).astype(BF16)
    flat = jnp.dot(upper, spread, preferred_element_type=F32) + jnp.dot(lower, spread, preferred_element_type=F32)

    for pair in range(PAIRS):

        @pl.loop(1, plane)
        def _(slot):
            back(pair, slot).wait_recv()

        cols = slice(pair * 128, (pair + 1) * 128)
        scale = flat[:, cols].reshape(plane, tokens, 128)
        part = obuf[pair, 0].astype(F32) * scale[0]
        part = part + jnp.sum(rbuf[pair, 1:plane].astype(F32) * scale[1:], axis=0)
        result[0, :, cols] = part.astype(BF16)

    @pl.loop(1, plane)
    def _(step):
        stat1(step).wait_send()
        stat_back(step).wait_send()

        @pl.loop(0, PAIRS)
        def _(pair):
            share(pair, step).wait_send()
            back(pair, step).wait_send()

    @pl.loop(1, depth)
    def _(step):
        stat2(step).wait_send()

    for buf, send, recv, way, length in chains:
        for step in range(length):
            hop(buf, send, recv, way, step).wait_send()


def hand_over(result, att, fresh_keys, fresh_values, sems):
    copies = [
        pltpu.make_async_copy(result.at[i], out, sems.at[i])
        for i, out in enumerate((att, fresh_keys, fresh_values))
    ]
    for copy in copies:
        copy.start()
    for copy in copies:
        copy.wait()


def on_device(plane, x, gain, bias, wq, wk, wv, k, v):
    depth = lax.axis_size("rows") // plane
    tokens = x.shape[0]
    rows = plane * tokens
    dma = pltpu.SemaphoreType.DMA
    anywhere = pl.BlockSpec(memory_space=pltpu.HBM)
    local = pl.BlockSpec(memory_space=pltpu.VMEM)
    out = jax.ShapeDtypeStruct((tokens, WIDTH), BF16)
    result = pl.pallas_call(
        functools.partial(kernel, depth, plane, tokens),
        out_shape=pltpu.VMEM((3, tokens, WIDTH), BF16),
        in_specs=[anywhere, local, local] + [anywhere] * 5,
        out_specs=local,
        scratch_shapes=[
            pltpu.VMEM((tokens, CHANNELS), BF16),
            pltpu.VMEM((depth + 1, tokens, WIDTH), BF16),
            pltpu.VMEM((depth + 1, tokens, WIDTH), BF16),
            pltpu.VMEM((CHANNELS, WIDTH), BF16),
            pltpu.VMEM((CHANNELS, WIDTH), BF16),
            pltpu.VMEM((CHANNELS, WIDTH), BF16),
            pltpu.VMEM((CHANNELS, 128), BF16),
            pltpu.VMEM((PAIRS, plane, tokens, 128), BF16),
            pltpu.VMEM((plane, 2, 128), F32),
            pltpu.VMEM((depth, 2, 128), F32),
            pltpu.VMEM((PAIRS, rows, 128), F32),
            pltpu.VMEM((PAIRS, rows, 128), F32),
            pltpu.VMEM((PAIRS, rows, 128), F32),
            pltpu.VMEM((PAIRS, plane, tokens, 128), BF16),
            pltpu.VMEM((PAIRS, plane, tokens, 128), BF16),
            pltpu.VMEM((rows, 128), F32),
            pltpu.VMEM((plane, 8, 128), F32),
            pltpu.VMEM((plane, 8, 128), F32),
            dma((6,)),
            dma((plane,)), dma((plane,)), dma((depth,)), dma((depth,)),
            dma((PAIRS, plane)), dma((PAIRS, plane)),
            dma((2, depth)), dma((depth + 1,)), dma((2, depth)), dma((depth + 1,)),
            dma((PAIRS, plane)), dma((PAIRS, plane)),
            dma((plane,)), dma((plane,)),
        ],
        compiler_params=pltpu.CompilerParams(
            collective_id=0, has_side_effects=True, vmem_limit_bytes=60 * 1024 * 1024
        ),
        name="attention_of_plane",
    )(x, gain, bias, wq, wk, wv, k, v)
    return pl.pallas_call(
        hand_over,
        out_shape=(out, out, out),
        in_specs=[local],
        out_specs=(anywhere,) * 3,
        scratch_shapes=[dma((3,))],
        name="hand_over",
    )(result)


def solution(mesh, plane=PLANE):
    split = P(("batch", "rows"), None)
    return jax.shard_map(
        functools.partial(on_device, plane),
        mesh=mesh,
        in_specs=(split, P(), P(), P(), P(), P(), split, split),
        out_specs=(split, split, split),
        check_vma=False,
    )
```

time: 1280 us -> 62.1 us (0.05)
  blocking collectives: 1210 us -> 0 us
  Pallas kernels: 0 us -> 60.6 us
  local copies, waits for them, and re-layouts: 26.3 us -> 0.63 us
  matrix products: 14.1 us -> 0 us
  between operations: 14.2 us -> 0.65 us
    psum x2 -> x0, blocking collectives: 1210 us -> none  [the longest x1 609 us: on_device(): sums = lax.psum(jnp.sum(widened, axis=0), 'rows')]
    pallas_call x0 -> x2, Pallas kernels: none -> 60.6 us  [the longest x1 59 us: on_device(): pl.pallas_call(functools.partial(kernel, depth, plane, tokens), out_shape...]
    all_gather x2 -> x0, local copies, waits for them, and re-layouts: 15.8 us -> none  [the longest x1 7.89 us: on_device(): lax.all_gather(stale_keys, 'rows', axis=0, tiled=True)]
    dot_general x5 -> x0, matrix products: 14.1 us -> none  [the longest x1 5.65 us: head_values(): jnp.einsum('qhk,khd->qhd', exps.astype(jnp.bfloat16), values_three, prefe...]
  transfers between devices with their start and end apart: 2 -> 0, of which waited for: 0 -> 0; matrix products, arithmetic and copies ran while one was open for 2% -> 0% of each run, Pallas kernels for 0% -> 0%
where the time goes in v1:
time: 62.1 us; the launch traced here: 61.9 us
  Pallas kernels  60.6 us (98%)
  between operations  0.65 us (1%)
  local copies, waits for them, and re-layouts  0.63 us (1%)
    pallas_call x1, Pallas kernels, on_device(): pl.pallas_call(functools.partial(kernel, depth, plane, tokens), out_shape...  59 us
    pallas_call x1, Pallas kernels, on_device(): pl.pallas_call(hand_over, out_shape=(out, out, out), in_specs=[local], ou...  1.57 us

profile of v1, /device:TPU:6, one launch (start us, length us, event | category | flops | bytes accessed | tf_op | source)
XLA Modules:
  0.0 61.9 jit_solution(6779346580865916635)
XLA Ops:
  0.6 59.0 %attention_of_plane.1.result = bf16[3,32,640]{2,1,0:T(8,128)(2,1)S(1)} custom-call(bf16[32,1280]{1,0:T(8,128)(2,1)} %x_in.1, f32[1280]{0:T(1024)} %gain.1, f32[1280]{0:T(1024)} %bias.1, bf16[1280,640]{1,0:T(8,128)(2,1)} %wq_in.1, bf16[1280,640]{1,0:T(8,128)(2,1)} %wk_in.1, bf16[1280,640]{1,0:T(8,128)(2,1)} %wv_in.1, bf16[32,640]{1,0:T(8,128)(2,1)} %k_in.1, ...), custom_call_target="tpu_custom_call" | custom-call | tf_op jit(solution)/shard_map/attention_of_plane/pallas_call | solution.py:379
  59.7 0.0 copy-start
  59.7 0.6 %copy-done = bf16[3,32,640]{2,1,0:T(8,128)(2,1)} copy-done((bf16[3,32,640]{2,1,0:T(8,128)(2,1)}, bf16[3,32,640]{2,1,0:T(8,128)(2,1)S(1)}, u32[]{:S(2)}) %copy-start) | copy-done | bytes 122904
  60.3 1.6 %hand_over.1 = (bf16[32,640]{1,0:T(8,128)(2,1)}, bf16[32,640]{1,0:T(8,128)(2,1)}, bf16[32,640]{1,0:T(8,128)(2,1)}) custom-call(bf16[3,32,640]{2,1,0:T(8,128)(2,1)} %copy-done), custom_call_target="tpu_custom_call" | custom-call | tf_op jit(solution)/shard_map/hand_over/pallas_call | solution.py:415
Async XLA Ops:
  59.7 0.6 %copy-start = (bf16[3,32,640]{2,1,0:T(8,128)(2,1)}, bf16[3,32,640]{2,1,0:T(8,128)(2,1)S(1)}, u32[]{:S(2)}) copy-start(bf16[3,32,640]{2,1,0:T(8,128)(2,1)S(1)} %attention_of_plane.1.result) | copy-start | bytes 368644

commit v2 on v1

--- a/solution.py
+++ b/solution.py
@@ -105,16 +105,19 @@
     pl.semaphore_wait(barrier, plane + depth - 2)
 
     def stat1(step):
-        return remote(st1.at[0], st1.at[step], s1_send.at[step], s1_recv.at[step], in_plane(step))
+        return remote(st1.at[0], st1.at[step], s1_send, s1_recv, in_plane(step))
 
     def stat2(step):
-        return remote(st2.at[0], st2.at[step], s2_send.at[step], s2_recv.at[step], in_depth(step))
+        return remote(st2.at[0], st2.at[step], s2_send, s2_recv, in_depth(step))
 
     def share(pair, step):
         return remote(
-            qbuf.at[pair, 0], qbuf.at[pair, step], q_send.at[pair, step], q_recv.at[pair, step],
-            in_plane(step),
+            qbuf.at[pair, 0], qbuf.at[pair, step], q_send.at[pair], q_recv.at[pair], in_plane(step)
         )
+
+    def all_of(buf, send, recv):
+        rest = buf.at[pl.ds(1, buf.shape[0] - 1)]
+        return remote(rest, rest, send, recv, in_plane(1))
 
     order = [0]
     for step in range(1, half):
@@ -123,13 +126,12 @@
     middle = half
     place = {block: at if at < middle else at + 1 for at, block in enumerate(order)}
 
-    def hop(buf, send, recv, way, step):
-        if way == 0:
-            ends, device = (step, step + 1), in_depth(1)
-        else:
-            ends, device = ((depth - step) % depth, depth - step - 1), in_depth(depth - 1)
+    def hop(buf, send, recv, way, distance):
+        before = distance - 1 if distance % 2 else distance - 2
+        ends = [at if way == 0 else (depth - at) % depth for at in (before, distance)]
+        by = distance - before if way == 0 else depth - (distance - before)
         here, there = place[ends[0]], place[ends[1]]
-        return remote(buf.at[here], buf.at[there], send.at[way, step], recv.at[there], device)
+        return remote(buf.at[here], buf.at[there], send.at[way, distance], recv.at[there], in_depth(by))
 
     chains = [
         (kbuf, k_send, k_recv, 0, half),
@@ -138,17 +140,24 @@
         (vbuf, v_send, v_recv, 0, half - 1),
     ]
 
-    def ring(step):
-        for buf, send, recv, way, length in chains:
-            if step <= length:
-                if step > 0:
-                    hop(buf, send, recv, way, step - 1).wait_recv()
-                if step < length:
-                    hop(buf, send, recv, way, step).start()
-
-    def rings(first, last):
-        for step in range(first, min(last, half) + 1):
-            ring(step)
+    here_already = {0}
+
+    def arrive(first, last):
+        for distance in sorted(min(block, depth - block) for block in order[first:last]):
+            if distance not in here_already:
+                here_already.add(distance)
+                for *chain, length in chains:
+                    if distance <= length:
+                        hop(*chain, distance).wait_recv()
+
+    def forward(stop):
+        here_already.add(stop)
+        for *chain, length in chains:
+            if 0 < stop <= length:
+                hop(*chain, stop).wait_recv()
+            for distance in (stop + 2, stop + 1):
+                if distance <= length:
+                    hop(*chain, distance).start()
 
     def merged(stats):
         means, spread = stats[:, 0, :], stats[:, 1, :]
@@ -160,11 +169,8 @@
     def _(step):
         stat1(step).start()
 
-    rings(0, 0)
-
-    @pl.loop(1, plane)
-    def _(step):
-        stat1(step).wait_recv()
+    forward(0)
+    all_of(st1, s1_send, s1_recv).wait_recv()
 
     mean, var = merged(st1[...])
     st2[0, 0:1, :] = mean
@@ -174,11 +180,8 @@
     def _(step):
         stat2(step).start()
 
-    rings(1, 1)
-
-    @pl.loop(1, depth)
-    def _(step):
-        stat2(step).wait_recv()
+    forward(2)
+    all_of(st2, s2_send, s2_recv).wait_recv()
 
     mean, var = merged(st2[...])
     line = lax.broadcasted_iota(jnp.int32, (8, 128), 0)
@@ -188,7 +191,6 @@
     bias_chan = bias[...].reshape(1, CHANNELS)
     normed = ((x_own[...].astype(F32) - mean_chan) * scale_chan + bias_chan).astype(BF16)
 
-    rings(2, 2)
     loads[3].wait()
     query = jnp.dot(normed, wq[...], preferred_element_type=F32).astype(BF16)
     query = query * jnp.asarray(HEAD_DIM**-0.5, BF16)
@@ -201,12 +203,11 @@
         def _(step):
             share(pair, step).start()
 
-    rings(3, 3)
+    forward(4)
     loads[4].wait()
     fresh = jnp.dot(normed, wk[...], preferred_element_type=F32).astype(BF16)
     kbuf[middle] = fresh
     result[1] = fresh
-    rings(4, 4)
     loads[5].wait()
     fresh = jnp.dot(normed, wv[...], preferred_element_type=F32).astype(BF16)
     vbuf[middle] = fresh
@@ -215,13 +216,13 @@
     lane = lax.broadcasted_iota(jnp.int32, (1, 128), 1)
     low = lane < HEAD_DIM
     masks = (jnp.where(low, 1.0, 0.0).astype(BF16), jnp.where(low, 0.0, 1.0).astype(BF16))
-    keys_len = half * tokens
-    ones = jnp.ones((keys_len, 128), BF16)
-
-    def attend(query, start, pair):
+
+    def attend(query, start, blocks, pair):
         cols = pl.ds(pl.multiple_of(pair * 128, 128), 128)
-        keys = kbuf[start : start + half, :, cols].reshape(keys_len, 128)
-        values = vbuf[start : start + half, :, cols].reshape(keys_len, 128)
+        keys_len = blocks * tokens
+        keys = kbuf[start : start + blocks, :, cols].reshape(keys_len, 128)
+        values = vbuf[start : start + blocks, :, cols].reshape(keys_len, 128)
+        ones = jnp.ones((keys_len, 128), BF16)
         count = query.shape[0]
         both = jnp.concatenate([query * masks[0], query * masks[1]], axis=0)
         scores = lax.dot_general(both, keys, NT, preferred_element_type=F32)
@@ -238,51 +239,59 @@
         for buf, value in zip((part_o, part_m, part_l), parts):
             buf[pair, first:last] = value
 
-    rows = plane * tokens
-
-    @pl.loop(0, PAIRS)
-    def _(pair):
-        keep(pair, 0, tokens, attend(qbuf[pair, 0], 1, pair))
-
-    rings(5, 6)
-
-    def first_half(pair):
-        @pl.loop(1, plane)
-        def _(step):
-            share(pair, step).wait_recv()
-
-        others = qbuf[pair, 1:plane].reshape(rows - tokens, 128)
-        keep(pair, tokens, rows, attend(others, 0, pair))
-
-    pl.loop(0, 2)(first_half)
-    rings(7, 7)
-    pl.loop(2, PAIRS)(first_half)
-    rings(8, half)
-
-    def back(pair, slot):
-        return remote(
-            obuf.at[pair, slot], rbuf.at[pair, slot], o_send.at[pair, slot], o_recv.at[pair, slot],
-            in_plane(plane - slot),
-        )
-
-    def stat_back(slot):
-        return remote(
-            ostat_packed.at[slot], rstat_packed.at[slot], t_send.at[slot], t_recv.at[slot],
-            in_plane(plane - slot),
-        )
-
-    ostat[...] = jnp.zeros_like(ostat)
-    within = lax.rem(lane, HEAD_DIM)
-
-    @pl.loop(0, PAIRS)
-    def _(pair):
-        out, largest, total = attend(qbuf[pair].reshape(rows, 128), half + 1, pair)
+    def add_to(pair, parts):
+        out, largest, total = parts
         old_largest = part_m[pair]
         top = jnp.maximum(largest, old_largest)
         now, before = jnp.exp(largest - top), jnp.exp(old_largest - top)
-        out = (out * now + part_o[pair] * before).astype(BF16)
-        total = total * now + part_l[pair] * before
-        obuf[pair] = out.reshape(plane, tokens, 128)
+        return out * now + part_o[pair] * before, top, total * now + part_l[pair] * before
+
+    rows = plane * tokens
+    quarter = half // 2
+
+    arrive(0, half)
+
+    @pl.loop(0, PAIRS)
+    def _(pair):
+        keep(pair, 0, tokens, attend(qbuf[pair, 0], 1, half, pair))
+
+    def first_half(pair):
+        all_of(qbuf.at[pair], q_send.at[pair], q_recv.at[pair]).wait_recv()
+        others = qbuf[pair, 1:plane].reshape(rows - tokens, 128)
+        keep(pair, tokens, rows, attend(others, 0, half, pair))
+
+    pl.loop(0, 2)(first_half)
+    if half > 4:
+        forward(6)
+    pl.loop(2, PAIRS)(first_half)
+    arrive(half, half + quarter)
+
+    @pl.loop(0, PAIRS)
+    def _(pair):
+        parts = attend(qbuf[pair].reshape(rows, 128), half + 1, quarter, pair)
+        keep(pair, 0, rows, add_to(pair, parts))
+
+    arrive(half + quarter, depth)
+
+    def back(pair, slot):
+        return remote(
+            obuf.at[pair, slot], rbuf.at[pair, slot], o_send.at[pair], o_recv.at[pair],
+            in_plane(plane - slot),
+        )
+
+    def stat_back(slot):
+        return remote(
+            ostat_packed.at[slot], rstat_packed.at[slot], t_send, t_recv, in_plane(plane - slot)
+        )
+
+    ostat[...] = jnp.zeros_like(ostat)
+    within = lax.rem(lane, HEAD_DIM)
+
+    @pl.loop(0, PAIRS)
+    def _(pair):
+        parts = attend(qbuf[pair].reshape(rows, 128), half + 1 + quarter, quarter, pair)
+        out, top, total = add_to(pair, parts)
+        obuf[pair] = out.astype(BF16).reshape(plane, tokens, 128)
 
         @pl.loop(1, plane)
         def _(slot):
@@ -309,10 +318,15 @@
     spread = jnp.where((feature >= from_feature) & (feature < from_feature + HEAD_DIM), 1.0, 0.0).astype(BF16)
     rstat_packed[0] = ostat_packed[0]
 
-    @pl.loop(1, plane)
-    def _(slot):
-        stat_back(slot).wait_recv()
-
+    all_of(st1, s1_send, s1_recv).wait_send()
+    all_of(st2, s2_send, s2_recv).wait_send()
+    for *chain, length in chains:
+        for distance in range(1, length + 1):
+            hop(*chain, distance).wait_send()
+    for pair in range(PAIRS):
+        all_of(qbuf.at[pair], q_send.at[pair], q_recv.at[pair]).wait_send()
+
+    all_of(rstat_packed, t_send, t_recv).wait_recv()
     packed = rstat_packed[...].reshape(plane * 8, 128)
     tiles = [pltpu.roll(packed, 128 - 16 * pack, 1) if pack else packed for pack in range(packs)]
     stats = jnp.concatenate([tile.reshape(plane, 8, 128) for tile in tiles], axis=1)
@@ -327,34 +341,16 @@
     flat = jnp.dot(upper, spread, preferred_element_type=F32) + jnp.dot(lower, spread, preferred_element_type=F32)
 
     for pair in range(PAIRS):
-
-        @pl.loop(1, plane)
-        def _(slot):
-            back(pair, slot).wait_recv()
-
+        all_of(rbuf.at[pair], o_send.at[pair], o_recv.at[pair]).wait_recv()
         cols = slice(pair * 128, (pair + 1) * 128)
         scale = flat[:, cols].reshape(plane, tokens, 128)
         part = obuf[pair, 0].astype(F32) * scale[0]
         part = part + jnp.sum(rbuf[pair, 1:plane].astype(F32) * scale[1:], axis=0)
         result[0, :, cols] = part.astype(BF16)
 
-    @pl.loop(1, plane)
-    def _(step):
-        stat1(step).wait_send()
-        stat_back(step).wait_send()
-
-        @pl.loop(0, PAIRS)
-        def _(pair):
-            share(pair, step).wait_send()
-            back(pair, step).wait_send()
-
-    @pl.loop(1, depth)
-    def _(step):
-        stat2(step).wait_send()
-
-    for buf, send, recv, way, length in chains:
-        for step in range(length):
-            hop(buf, send, recv, way, step).wait_send()
+    for pair in range(PAIRS):
+        all_of(obuf.at[pair], o_send.at[pair], o_recv.at[pair]).wait_send()
+    all_of(ostat_packed, t_send, t_recv).wait_send()
 
 
 def hand_over(result, att, fresh_keys, fresh_values, sems):
@@ -401,11 +397,11 @@
             pltpu.VMEM((plane, 8, 128), F32),
             pltpu.VMEM((plane, 8, 128), F32),
             dma((6,)),
-            dma((plane,)), dma((plane,)), dma((depth,)), dma((depth,)),
-            dma((PAIRS, plane)), dma((PAIRS, plane)),
+            dma, dma, dma, dma,
+            dma((PAIRS,)), dma((PAIRS,)),
             dma((2, depth)), dma((depth + 1,)), dma((2, depth)), dma((depth + 1,)),
-            dma((PAIRS, plane)), dma((PAIRS, plane)),
-            dma((plane,)), dma((plane,)),
+            dma((PAIRS,)), dma((PAIRS,)),
+            dma, dma,
         ],
         compiler_params=pltpu.CompilerParams(
             collective_id=0, has_side_effects=True, vmem_limit_bytes=60 * 1024 * 1024
@@ -419,7 +415,7 @@
         out_specs=(anywhere,) * 3,
         scratch_shapes=[dma((3,))],
         name="hand_over",
-    )(result)
+    )(pltpu.with_memory_space_constraint(result, pltpu.VMEM))
 
 
 def solution(mesh, plane=PLANE):

time: 62.1 us -> 50.9 us (0.82)
  Pallas kernels: 60.6 us -> 49.7 us
  local copies, waits for them, and re-layouts: 0.63 us -> 0 us
    pallas_call x1, Pallas kernels: 59 us -> 49 us  [on_device(): pl.pallas_call(functools.partial(kernel, depth, plane, tokens), out_shape...]
    pallas_call x1, Pallas kernels: 1.57 us -> 0.67 us  [on_device(): pl.pallas_call(hand_over, out_shape=(out, out, out), in_specs=[local], ou...]
    unnamed x2 -> x0, local copies, waits for them, and re-layouts: 0.63 us -> none
where the time goes in v2:
time: 50.9 us; the launch traced here: 50.3 us
  Pallas kernels  49.7 us (98%)
  between operations  0.64 us (1%)
    pallas_call x1, Pallas kernels, on_device(): pl.pallas_call(functools.partial(kernel, depth, plane, tokens), out_shape...  49 us

profile of v2, /device:TPU:6, one launch (start us, length us, event | category | flops | bytes accessed | tf_op | source)
XLA Modules:
  0.0 50.3 jit_solution(12376203374340488118)
XLA Ops:
  0.6 49.0 %attention_of_plane.1.result = bf16[3,32,640]{2,1,0:T(8,128)(2,1)S(1)} custom-call(bf16[32,1280]{1,0:T(8,128)(2,1)} %x_in.1, f32[1280]{0:T(1024)} %gain.1, f32[1280]{0:T(1024)} %bias.1, bf16[1280,640]{1,0:T(8,128)(2,1)} %wq_in.1, bf16[1280,640]{1,0:T(8,128)(2,1)} %wk_in.1, bf16[1280,640]{1,0:T(8,128)(2,1)} %wv_in.1, bf16[32,640]{1,0:T(8,128)(2,1)} %k_in.1, ...), custom_call_target="tpu_custom_call" | custom-call | tf_op jit(solution)/shard_map/attention_of_plane/pallas_call | solution.py:375
  49.6 0.7 %hand_over.1 = (bf16[32,640]{1,0:T(8,128)(2,1)}, bf16[32,640]{1,0:T(8,128)(2,1)}, bf16[32,640]{1,0:T(8,128)(2,1)}) custom-call(bf16[3,32,640]{2,1,0:T(8,128)(2,1)S(1)} %attention_of_plane.1.result), custom_call_target="tpu_custom_call" | custom-call | tf_op jit(solution)/shard_map/hand_over/pallas_call | solution.py:411

commit v3 on v2

--- a/solution.py
+++ b/solution.py
@@ -77,7 +77,7 @@
     loads = [
         pltpu.make_async_copy(src, dst, in_sem.at[i])
         for i, (src, dst) in enumerate(
-            [(x_in, x_own), (k_in, kbuf.at[0]), (v_in, vbuf.at[0]),
+            [(k_in, kbuf.at[0]), (v_in, vbuf.at[0]), (x_in, x_own),
              (wq_in, wq), (wk_in, wk), (wv_in, wv)]
         )
     ]
@@ -91,6 +91,73 @@
     member[...] = jnp.where(inside, 1.0, 0.0).astype(BF16)
 
     loads[0].wait()
+    loads[1].wait()
+    pl.semaphore_wait(barrier, plane + depth - 2)
+
+    def stat1(step):
+        return remote(st1.at[0], st1.at[step], s1_send, s1_recv, in_plane(step))
+
+    def stat2(step):
+        return remote(st2.at[0], st2.at[step], s2_send, s2_recv, in_depth(step))
+
+    def share(pair, step):
+        return remote(
+            qbuf.at[pair, 0], qbuf.at[pair, step], q_send.at[pair], q_recv.at[pair], in_plane(step)
+        )
+
+    def all_of(buf, send, recv):
+        rest = buf.at[pl.ds(1, buf.shape[0] - 1)]
+        return remote(rest, rest, send, recv, in_plane(1))
+
+    order = [0]
+    for step in range(1, half):
+        order += [step, depth - step]
+    order += [half]
+    middle = half
+    place = {block: at if at < middle else at + 1 for at, block in enumerate(order)}
+
+    def hop(buf, send, recv, way, distance):
+        before = distance - 1 if distance % 2 else distance - 2
+        ends = [at if way == 0 else (depth - at) % depth for at in (before, distance)]
+        by = distance - before if way == 0 else depth - (distance - before)
+        here, there = place[ends[0]], place[ends[1]]
+        return remote(buf.at[here], buf.at[there], send.at[way, distance], recv.at[there], in_depth(by))
+
+    chains = [
+        (kbuf, k_send, k_recv, 0, half),
+        (vbuf, v_send, v_recv, 1, half),
+        (kbuf, k_send, k_recv, 1, half - 1),
+        (vbuf, v_send, v_recv, 0, half - 1),
+    ]
+
+    here_already = {0}
+
+    def arrive(first, last):
+        for distance in sorted(min(block, depth - block) for block in order[first:last]):
+            if distance not in here_already:
+                here_already.add(distance)
+                for *chain, length in chains:
+                    if distance <= length:
+                        hop(*chain, distance).wait_recv()
+
+    def forward(stop):
+        here_already.add(stop)
+        for *chain, length in chains:
+            if 0 < stop <= length:
+                hop(*chain, stop).wait_recv()
+            for distance in (stop + 2, stop + 1):
+                if distance <= length:
+                    hop(*chain, distance).start()
+
+    def merged(stats):
+        means, spread = stats[:, 0, :], stats[:, 1, :]
+        mean = jnp.mean(means, axis=0, keepdims=True)
+        apart = means - mean
+        return mean, jnp.mean(spread + apart * apart, axis=0, keepdims=True)
+
+    forward(0)
+
+    loads[2].wait()
     x = x_own[...]
     count = tokens * GROUP_WIDTH
     mean = jnp.sum(jnp.dot(x, member[...], preferred_element_type=F32), axis=0, keepdims=True) / count
@@ -99,77 +166,11 @@
     var = jnp.sum(to_groups(squares, member[...]), axis=0, keepdims=True) / count
     st1[0, 0:1, :] = mean
     st1[0, 1:2, :] = var
-    loads[1].wait()
-    loads[2].wait()
-
-    pl.semaphore_wait(barrier, plane + depth - 2)
-
-    def stat1(step):
-        return remote(st1.at[0], st1.at[step], s1_send, s1_recv, in_plane(step))
-
-    def stat2(step):
-        return remote(st2.at[0], st2.at[step], s2_send, s2_recv, in_depth(step))
-
-    def share(pair, step):
-        return remote(
-            qbuf.at[pair, 0], qbuf.at[pair, step], q_send.at[pair], q_recv.at[pair], in_plane(step)
-        )
-
-    def all_of(buf, send, recv):
-        rest = buf.at[pl.ds(1, buf.shape[0] - 1)]
-        return remote(rest, rest, send, recv, in_plane(1))
-
-    order = [0]
-    for step in range(1, half):
-        order += [step, depth - step]
-    order += [half]
-    middle = half
-    place = {block: at if at < middle else at + 1 for at, block in enumerate(order)}
-
-    def hop(buf, send, recv, way, distance):
-        before = distance - 1 if distance % 2 else distance - 2
-        ends = [at if way == 0 else (depth - at) % depth for at in (before, distance)]
-        by = distance - before if way == 0 else depth - (distance - before)
-        here, there = place[ends[0]], place[ends[1]]
-        return remote(buf.at[here], buf.at[there], send.at[way, distance], recv.at[there], in_depth(by))
-
-    chains = [
-        (kbuf, k_send, k_recv, 0, half),
-        (vbuf, v_send, v_recv, 1, half),
-        (kbuf, k_send, k_recv, 1, half - 1),
-        (vbuf, v_send, v_recv, 0, half - 1),
-    ]
-
-    here_already = {0}
-
-    def arrive(first, last):
-        for distance in sorted(min(block, depth - block) for block in order[first:last]):
-            if distance not in here_already:
-                here_already.add(distance)
-                for *chain, length in chains:
-                    if distance <= length:
-                        hop(*chain, distance).wait_recv()
-
-    def forward(stop):
-        here_already.add(stop)
-        for *chain, length in chains:
-            if 0 < stop <= length:
-                hop(*chain, stop).wait_recv()
-            for distance in (stop + 2, stop + 1):
-                if distance <= length:
-                    hop(*chain, distance).start()
-
-    def merged(stats):
-        means, spread = stats[:, 0, :], stats[:, 1, :]
-        mean = jnp.mean(means, axis=0, keepdims=True)
-        apart = means - mean
-        return mean, jnp.mean(spread + apart * apart, axis=0, keepdims=True)
 
     @pl.loop(1, plane)
     def _(step):
         stat1(step).start()
 
-    forward(0)
     all_of(st1, s1_send, s1_recv).wait_recv()
 
     mean, var = merged(st1[...])
@@ -217,23 +218,34 @@
     low = lane < HEAD_DIM
     masks = (jnp.where(low, 1.0, 0.0).astype(BF16), jnp.where(low, 0.0, 1.0).astype(BF16))
 
-    def attend(query, start, blocks, pair):
-        cols = pl.ds(pl.multiple_of(pair * 128, 128), 128)
-        keys_len = blocks * tokens
-        keys = kbuf[start : start + blocks, :, cols].reshape(keys_len, 128)
-        values = vbuf[start : start + blocks, :, cols].reshape(keys_len, 128)
-        ones = jnp.ones((keys_len, 128), BF16)
-        count = query.shape[0]
+    def columns(buf, start, blocks, pair):
+        return buf[start : start + blocks, :, pair * 128 : (pair + 1) * 128].reshape(blocks * tokens, 128)
+
+    def scored(query, start, blocks, pair):
         both = jnp.concatenate([query * masks[0], query * masks[1]], axis=0)
+        keys = columns(kbuf, start, blocks, pair)
         scores = lax.dot_general(both, keys, NT, preferred_element_type=F32)
         largest = jnp.max(scores, axis=-1, keepdims=True)
-        exps = jnp.exp(scores - largest).astype(BF16)
-        sums = jnp.dot(exps, jnp.concatenate([values, ones], axis=1), preferred_element_type=F32)
+        return jnp.exp(scores - largest).astype(BF16), largest
+
+    def valued(exps, largest, start, blocks, pair):
+        ones = jnp.ones((blocks * tokens, 128), BF16)
+        right = jnp.concatenate([columns(vbuf, start, blocks, pair), ones], axis=1)
+        sums = jnp.dot(exps, right, preferred_element_type=F32)
+        count = exps.shape[0] // 2
 
         def pick(tall):
             return jnp.where(low, tall[0:count], tall[count:])
 
         return pick(sums[:, 0:128]), pick(jnp.broadcast_to(largest, (2 * count, 128))), pick(sums[:, 128:])
+
+    def attend(query_of, start, blocks, pairs, take):
+        waiting = None
+        for pair in list(pairs) + [None]:
+            ready = waiting
+            waiting = None if pair is None else (*scored(query_of(pair), start, blocks, pair), start, blocks, pair)
+            if ready is not None:
+                take(ready[-1], valued(*ready))
 
     def keep(pair, first, last, parts):
         for buf, value in zip((part_o, part_m, part_l), parts):
@@ -251,26 +263,32 @@
 
     arrive(0, half)
 
-    @pl.loop(0, PAIRS)
-    def _(pair):
-        keep(pair, 0, tokens, attend(qbuf[pair, 0], 1, half, pair))
-
-    def first_half(pair):
-        all_of(qbuf.at[pair], q_send.at[pair], q_recv.at[pair]).wait_recv()
-        others = qbuf[pair, 1:plane].reshape(rows - tokens, 128)
-        keep(pair, tokens, rows, attend(others, 0, half, pair))
-
-    pl.loop(0, 2)(first_half)
+    attend(
+        lambda pair: qbuf[pair, 0], 1, half, range(PAIRS),
+        lambda pair, parts: keep(pair, 0, tokens, parts),
+    )
+
+    def first_half(pairs):
+        for pair in pairs:
+            all_of(qbuf.at[pair], q_send.at[pair], q_recv.at[pair]).wait_recv()
+        attend(
+            lambda pair: qbuf[pair, 1:plane].reshape(rows - tokens, 128), 0, half, pairs,
+            lambda pair, parts: keep(pair, tokens, rows, parts),
+        )
+
+    first_half(range(0, 2))
     if half > 4:
         forward(6)
-    pl.loop(2, PAIRS)(first_half)
+    first_half(range(2, PAIRS))
     arrive(half, half + quarter)
 
-    @pl.loop(0, PAIRS)
-    def _(pair):
-        parts = attend(qbuf[pair].reshape(rows, 128), half + 1, quarter, pair)
-        keep(pair, 0, rows, add_to(pair, parts))
-
+    def all_queries(pair):
+        return qbuf[pair].reshape(rows, 128)
+
+    attend(
+        all_queries, half + 1, quarter, range(PAIRS),
+        lambda pair, parts: keep(pair, 0, rows, add_to(pair, parts)),
+    )
     arrive(half + quarter, depth)
 
     def back(pair, slot):
@@ -287,18 +305,15 @@
     ostat[...] = jnp.zeros_like(ostat)
     within = lax.rem(lane, HEAD_DIM)
 
-    @pl.loop(0, PAIRS)
-    def _(pair):
-        parts = attend(qbuf[pair].reshape(rows, 128), half + 1 + quarter, quarter, pair)
+    def send_back(pair, parts):
         out, top, total = add_to(pair, parts)
         obuf[pair] = out.astype(BF16).reshape(plane, tokens, 128)
-
-        @pl.loop(1, plane)
-        def _(slot):
+        for slot in range(1, plane):
             back(pair, slot).start()
-
         stats = jnp.where(within == pair, top, ostat[...])
         ostat[...] = jnp.where(within == pair + 8, total, stats)
+
+    attend(all_queries, half + 1 + quarter, quarter, range(PAIRS), send_back)
 
     packs = tokens // 8
     tiles = ostat[...].reshape(plane, packs, 8, 128)

time: 50.9 us -> 49.9 us (0.980)
  Pallas kernels: 49.7 us -> 48.7 us
    pallas_call x1, Pallas kernels: 49 us -> 48.1 us  [on_device(): pl.pallas_call(functools.partial(kernel, depth, plane, tokens), out_shape...]
where the time goes in v3:
time: 49.9 us; the launch traced here: 49.4 us
  Pallas kernels  48.7 us (98%)
  between operations  0.64 us (1%)
    pallas_call x1, Pallas kernels, on_device(): pl.pallas_call(functools.partial(kernel, depth, plane, tokens), out_shape...  48.1 us

profile of v3, /device:TPU:6, one launch (start us, length us, event | category | flops | bytes accessed | tf_op | source)
XLA Modules:
  0.0 49.4 jit_solution(8963380326122273375)
XLA Ops:
  0.6 48.1 %attention_of_plane.1.result = bf16[3,32,640]{2,1,0:T(8,128)(2,1)S(1)} custom-call(bf16[32,1280]{1,0:T(8,128)(2,1)} %x_in.1, f32[1280]{0:T(1024)} %gain.1, f32[1280]{0:T(1024)} %bias.1, bf16[1280,640]{1,0:T(8,128)(2,1)} %wq_in.1, bf16[1280,640]{1,0:T(8,128)(2,1)} %wk_in.1, bf16[1280,640]{1,0:T(8,128)(2,1)} %wv_in.1, bf16[32,640]{1,0:T(8,128)(2,1)} %k_in.1, ...), custom_call_target="tpu_custom_call" | custom-call | tf_op jit(solution)/shard_map/attention_of_plane/pallas_call | solution.py:390
  48.7 0.7 %hand_over.1 = (bf16[32,640]{1,0:T(8,128)(2,1)}, bf16[32,640]{1,0:T(8,128)(2,1)}, bf16[32,640]{1,0:T(8,128)(2,1)}) custom-call(bf16[3,32,640]{2,1,0:T(8,128)(2,1)S(1)} %attention_of_plane.1.result), custom_call_target="tpu_custom_call" | custom-call | tf_op jit(solution)/shard_map/hand_over/pallas_call | solution.py:426

commit v4 on v3

--- a/solution.py
+++ b/solution.py
@@ -43,10 +43,10 @@
     depth, plane, tokens,
     x_in, gain, bias, wq_in, wk_in, wv_in, k_in, v_in,
     result,
-    x_own, kbuf, vbuf, wq, wk, wv, member, qbuf, st1, st2,
+    x_own, kv, wq, wk, wv, member, qbuf, st1, st2,
     part_o, part_m, part_l, obuf, rbuf, ostat, ostat_packed, rstat_packed,
-    in_sem, s1_send, s1_recv, s2_send, s2_recv, q_send, q_recv,
-    k_send, k_recv, v_send, v_recv, o_send, o_recv, t_send, t_recv,
+    in_sem, kv_sem, s1_send, s1_recv, s2_send, s2_recv, q_send, q_recv,
+    kv_send, kv_recv, o_send, o_recv, t_send, t_recv,
 ):
     row = lax.axis_index("rows")
     z, p = row // plane, lax.rem(row, plane)
@@ -74,14 +74,16 @@
     def _(step):
         pl.semaphore_signal(barrier, inc=1, device_id=in_plane(step), device_id_type=MESH)
 
+    blocks_in = [
+        pltpu.make_async_copy(src.at[:, pl.ds(pair * 128, 128)], kv.at[0, pair, kind], kv_sem.at[pair, kind])
+        for pair in range(PAIRS)
+        for kind, src in enumerate((k_in, v_in))
+    ]
     loads = [
         pltpu.make_async_copy(src, dst, in_sem.at[i])
-        for i, (src, dst) in enumerate(
-            [(k_in, kbuf.at[0]), (v_in, vbuf.at[0]), (x_in, x_own),
-             (wq_in, wq), (wk_in, wk), (wv_in, wv)]
-        )
+        for i, (src, dst) in enumerate([(x_in, x_own), (wq_in, wq), (wk_in, wk), (wv_in, wv)])
     ]
-    for load in loads:
+    for load in blocks_in + loads:
         load.start()
 
     channel = lax.broadcasted_iota(jnp.int32, (CHANNELS, 128), 0)
@@ -90,8 +92,8 @@
     inside = (channel >= first) & (channel < first + GROUP_WIDTH) & (group < GROUPS)
     member[...] = jnp.where(inside, 1.0, 0.0).astype(BF16)
 
-    loads[0].wait()
-    loads[1].wait()
+    for load in blocks_in:
+        load.wait()
     pl.semaphore_wait(barrier, plane + depth - 2)
 
     def stat1(step):
@@ -116,38 +118,41 @@
     middle = half
     place = {block: at if at < middle else at + 1 for at, block in enumerate(order)}
 
-    def hop(buf, send, recv, way, distance):
+    def hop(way, pair, distance):
         before = distance - 1 if distance % 2 else distance - 2
         ends = [at if way == 0 else (depth - at) % depth for at in (before, distance)]
         by = distance - before if way == 0 else depth - (distance - before)
         here, there = place[ends[0]], place[ends[1]]
-        return remote(buf.at[here], buf.at[there], send.at[way, distance], recv.at[there], in_depth(by))
-
-    chains = [
-        (kbuf, k_send, k_recv, 0, half),
-        (vbuf, v_send, v_recv, 1, half),
-        (kbuf, k_send, k_recv, 1, half - 1),
-        (vbuf, v_send, v_recv, 0, half - 1),
-    ]
-
-    here_already = {0}
-
-    def arrive(first, last):
-        for distance in sorted(min(block, depth - block) for block in order[first:last]):
-            if distance not in here_already:
-                here_already.add(distance)
-                for *chain, length in chains:
-                    if distance <= length:
-                        hop(*chain, distance).wait_recv()
-
-    def forward(stop):
-        here_already.add(stop)
-        for *chain, length in chains:
-            if 0 < stop <= length:
-                hop(*chain, stop).wait_recv()
-            for distance in (stop + 2, stop + 1):
-                if distance <= length:
-                    hop(*chain, distance).start()
+        return remote(kv.at[here, pair], kv.at[there, pair], kv_send, kv_recv.at[there, pair], in_depth(by))
+
+    def length(way, pair):
+        return half if pair % 2 == way else half - 1
+
+    both_ways = (0, 1)
+    pairs_all = range(PAIRS)
+    seen = {(0, pair) for pair in pairs_all}
+
+    def arrive(distance, pair):
+        if (distance, pair) not in seen:
+            seen.add((distance, pair))
+            for way in both_ways:
+                if distance <= length(way, pair):
+                    hop(way, pair, distance).wait_recv()
+
+    def need(first, last, pairs):
+        for pair in pairs:
+            for distance in sorted(min(block, depth - block) for block in order[first:last]):
+                arrive(distance, pair)
+
+    def forward(stop, pairs):
+        if stop >= half:
+            return
+        for by in (2, 1):
+            for pair in pairs:
+                arrive(stop, pair)
+                for way in both_ways:
+                    if stop + by <= length(way, pair):
+                        hop(way, pair, stop + by).start()
 
     def merged(stats):
         means, spread = stats[:, 0, :], stats[:, 1, :]
@@ -155,9 +160,9 @@
         apart = means - mean
         return mean, jnp.mean(spread + apart * apart, axis=0, keepdims=True)
 
-    forward(0)
-
-    loads[2].wait()
+    forward(0, pairs_all)
+
+    loads[0].wait()
     x = x_own[...]
     count = tokens * GROUP_WIDTH
     mean = jnp.sum(jnp.dot(x, member[...], preferred_element_type=F32), axis=0, keepdims=True) / count
@@ -171,6 +176,7 @@
     def _(step):
         stat1(step).start()
 
+    forward(2, range(0, 2))
     all_of(st1, s1_send, s1_recv).wait_recv()
 
     mean, var = merged(st1[...])
@@ -181,10 +187,12 @@
     def _(step):
         stat2(step).start()
 
-    forward(2)
+    forward(2, range(2, PAIRS))
+    forward(4, range(0, 3))
     all_of(st2, s2_send, s2_recv).wait_recv()
 
     mean, var = merged(st2[...])
+    forward(4, range(3, PAIRS))
     line = lax.broadcasted_iota(jnp.int32, (8, 128), 0)
     wide = to_channels(jnp.where(line == 0, mean, lax.rsqrt(var + EPSILON)), member[...])
     mean_chan = wide[0:1]
@@ -192,7 +200,7 @@
     bias_chan = bias[...].reshape(1, CHANNELS)
     normed = ((x_own[...].astype(F32) - mean_chan) * scale_chan + bias_chan).astype(BF16)
 
-    loads[3].wait()
+    loads[1].wait()
     query = jnp.dot(normed, wq[...], preferred_element_type=F32).astype(BF16)
     query = query * jnp.asarray(HEAD_DIM**-0.5, BF16)
     for pair in range(PAIRS):
@@ -204,33 +212,37 @@
         def _(step):
             share(pair, step).start()
 
-    forward(4)
-    loads[4].wait()
+    forward(6, range(0, 3))
+    loads[2].wait()
     fresh = jnp.dot(normed, wk[...], preferred_element_type=F32).astype(BF16)
-    kbuf[middle] = fresh
+    for pair in range(PAIRS):
+        kv[middle, pair, 0] = fresh[:, pair * 128 : (pair + 1) * 128]
     result[1] = fresh
-    loads[5].wait()
+    loads[3].wait()
     fresh = jnp.dot(normed, wv[...], preferred_element_type=F32).astype(BF16)
-    vbuf[middle] = fresh
+    for pair in range(PAIRS):
+        kv[middle, pair, 1] = fresh[:, pair * 128 : (pair + 1) * 128]
     result[2] = fresh
+    forward(6, range(3, PAIRS))
+    need(0, half, pairs_all)
 
     lane = lax.broadcasted_iota(jnp.int32, (1, 128), 1)
     low = lane < HEAD_DIM
     masks = (jnp.where(low, 1.0, 0.0).astype(BF16), jnp.where(low, 0.0, 1.0).astype(BF16))
 
-    def columns(buf, start, blocks, pair):
-        return buf[start : start + blocks, :, pair * 128 : (pair + 1) * 128].reshape(blocks * tokens, 128)
+    def gathered(kind, start, blocks, pair):
+        return kv[start : start + blocks, pair, kind].reshape(blocks * tokens, 128)
 
     def scored(query, start, blocks, pair):
         both = jnp.concatenate([query * masks[0], query * masks[1]], axis=0)
-        keys = columns(kbuf, start, blocks, pair)
+        keys = gathered(0, start, blocks, pair)
         scores = lax.dot_general(both, keys, NT, preferred_element_type=F32)
         largest = jnp.max(scores, axis=-1, keepdims=True)
         return jnp.exp(scores - largest).astype(BF16), largest
 
     def valued(exps, largest, start, blocks, pair):
         ones = jnp.ones((blocks * tokens, 128), BF16)
-        right = jnp.concatenate([columns(vbuf, start, blocks, pair), ones], axis=1)
+        right = jnp.concatenate([gathered(1, start, blocks, pair), ones], axis=1)
         sums = jnp.dot(exps, right, preferred_element_type=F32)
         count = exps.shape[0] // 2
 
@@ -261,7 +273,6 @@
     rows = plane * tokens
     quarter = half // 2
 
-    arrive(0, half)
 
     attend(
         lambda pair: qbuf[pair, 0], 1, half, range(PAIRS),
@@ -277,10 +288,8 @@
         )
 
     first_half(range(0, 2))
-    if half > 4:
-        forward(6)
     first_half(range(2, PAIRS))
-    arrive(half, half + quarter)
+    need(half, half + quarter, pairs_all)
 
     def all_queries(pair):
         return qbuf[pair].reshape(rows, 128)
@@ -289,7 +298,10 @@
         all_queries, half + 1, quarter, range(PAIRS),
         lambda pair, parts: keep(pair, 0, rows, add_to(pair, parts)),
     )
-    arrive(half + quarter, depth)
+
+    def all_here(pair):
+        need(half + quarter, depth, [pair])
+        return all_queries(pair)
 
     def back(pair, slot):
         return remote(
@@ -313,7 +325,7 @@
         stats = jnp.where(within == pair, top, ostat[...])
         ostat[...] = jnp.where(within == pair + 8, total, stats)
 
-    attend(all_queries, half + 1 + quarter, quarter, range(PAIRS), send_back)
+    attend(all_here, half + 1 + quarter, quarter, range(PAIRS), send_back)
 
     packs = tokens // 8
     tiles = ostat[...].reshape(plane, packs, 8, 128)
@@ -335,9 +347,8 @@
 
     all_of(st1, s1_send, s1_recv).wait_send()
     all_of(st2, s2_send, s2_recv).wait_send()
-    for *chain, length in chains:
-        for distance in range(1, length + 1):
-            hop(*chain, distance).wait_send()
+    every = kv.at[pl.ds(0, depth - 1)]
+    remote(every, every, kv_send, kv_recv.at[0, 0], in_depth(1)).wait_send()
     for pair in range(PAIRS):
         all_of(qbuf.at[pair], q_send.at[pair], q_recv.at[pair]).wait_send()
 
@@ -394,8 +405,7 @@
         out_specs=local,
         scratch_shapes=[
             pltpu.VMEM((tokens, CHANNELS), BF16),
-            pltpu.VMEM((depth + 1, tokens, WIDTH), BF16),
-            pltpu.VMEM((depth + 1, tokens, WIDTH), BF16),
+            pltpu.VMEM((depth + 1, PAIRS, 2, tokens, 128), BF16),
             pltpu.VMEM((CHANNELS, WIDTH), BF16),
             pltpu.VMEM((CHANNELS, WIDTH), BF16),
             pltpu.VMEM((CHANNELS, WIDTH), BF16),
@@ -411,10 +421,10 @@
             pltpu.VMEM((rows, 128), F32),
             pltpu.VMEM((plane, 8, 128), F32),
             pltpu.VMEM((plane, 8, 128), F32),
-            dma((6,)),
+            dma((4,)), dma((PAIRS, 2)),
             dma, dma, dma, dma,
             dma((PAIRS,)), dma((PAIRS,)),
-            dma((2, depth)), dma((depth + 1,)), dma((2, depth)), dma((depth + 1,)),
+            dma, dma((depth + 1, PAIRS)),
             dma((PAIRS,)), dma((PAIRS,)),
             dma, dma,
         ],

time: 49.9 us -> 48 us (0.962)
  Pallas kernels: 48.7 us -> 46.8 us
    pallas_call x1, Pallas kernels: 48.1 us -> 46.1 us  [on_device(): pl.pallas_call(functools.partial(kernel, depth, plane, tokens), out_shape...]
where the time goes in v4:
time: 48 us; the launch traced here: 47.4 us
  Pallas kernels  46.8 us (98%)
  between operations  0.64 us (1%)
    pallas_call x1, Pallas kernels, on_device(): pl.pallas_call(functools.partial(kernel, depth, plane, tokens), out_shape...  46.1 us

profile of v4, /device:TPU:6, one launch (start us, length us, event | category | flops | bytes accessed | tf_op | source)
XLA Modules:
  0.0 47.4 jit_solution(1778579410710553666)
XLA Ops:
  0.6 46.1 %attention_of_plane.1.result = bf16[3,32,640]{2,1,0:T(8,128)(2,1)S(1)} custom-call(bf16[32,1280]{1,0:T(8,128)(2,1)} %x_in.1, f32[1280]{0:T(1024)} %gain.1, f32[1280]{0:T(1024)} %bias.1, bf16[1280,640]{1,0:T(8,128)(2,1)} %wq_in.1, bf16[1280,640]{1,0:T(8,128)(2,1)} %wk_in.1, bf16[1280,640]{1,0:T(8,128)(2,1)} %wv_in.1, bf16[32,640]{1,0:T(8,128)(2,1)} %k_in.1, ...), custom_call_target="tpu_custom_call" | custom-call | tf_op jit(solution)/shard_map/attention_of_plane/pallas_call | solution.py:401
  46.8 0.7 %hand_over.1 = (bf16[32,640]{1,0:T(8,128)(2,1)}, bf16[32,640]{1,0:T(8,128)(2,1)}, bf16[32,640]{1,0:T(8,128)(2,1)}) custom-call(bf16[3,32,640]{2,1,0:T(8,128)(2,1)S(1)} %attention_of_plane.1.result), custom_call_target="tpu_custom_call" | custom-call | tf_op jit(solution)/shard_map/hand_over/pallas_call | solution.py:436

commit v5 on v4

--- a/solution.py
+++ b/solution.py
@@ -43,9 +43,9 @@
     depth, plane, tokens,
     x_in, gain, bias, wq_in, wk_in, wv_in, k_in, v_in,
     result,
-    x_own, kv, wq, wk, wv, member, qbuf, st1, st2,
+    xbuf, kv, wq, wk, wv, member, nbuf, qbuf, st1, st2,
     part_o, part_m, part_l, obuf, rbuf, ostat, ostat_packed, rstat_packed,
-    in_sem, kv_sem, s1_send, s1_recv, s2_send, s2_recv, q_send, q_recv,
+    in_sem, kv_sem, s1_send, s1_recv, s2_send, s2_recv, x_send, x_recv,
     kv_send, kv_recv, o_send, o_recv, t_send, t_recv,
 ):
     row = lax.axis_index("rows")
@@ -81,7 +81,7 @@
     ]
     loads = [
         pltpu.make_async_copy(src, dst, in_sem.at[i])
-        for i, (src, dst) in enumerate([(x_in, x_own), (wq_in, wq), (wk_in, wk), (wv_in, wv)])
+        for i, (src, dst) in enumerate([(x_in, xbuf.at[0]), (wq_in, wq), (wk_in, wk), (wv_in, wv)])
     ]
     for load in blocks_in + loads:
         load.start()
@@ -102,10 +102,8 @@
     def stat2(step):
         return remote(st2.at[0], st2.at[step], s2_send, s2_recv, in_depth(step))
 
-    def share(pair, step):
-        return remote(
-            qbuf.at[pair, 0], qbuf.at[pair, step], q_send.at[pair], q_recv.at[pair], in_plane(step)
-        )
+    def share(step):
+        return remote(xbuf.at[0], xbuf.at[step], x_send, x_recv, in_plane(step))
 
     def all_of(buf, send, recv):
         rest = buf.at[pl.ds(1, buf.shape[0] - 1)]
@@ -144,10 +142,10 @@
             for distance in sorted(min(block, depth - block) for block in order[first:last]):
                 arrive(distance, pair)
 
-    def forward(stop, pairs):
+    def forward(stop, pairs, hops=(2, 1)):
         if stop >= half:
             return
-        for by in (2, 1):
+        for by in hops:
             for pair in pairs:
                 arrive(stop, pair)
                 for way in both_ways:
@@ -160,10 +158,12 @@
         apart = means - mean
         return mean, jnp.mean(spread + apart * apart, axis=0, keepdims=True)
 
-    forward(0, pairs_all)
-
+    forward(0, pairs_all, (2,))
     loads[0].wait()
-    x = x_own[...]
+    for step in range(1, plane):
+        share(step).start()
+
+    x = xbuf[0]
     count = tokens * GROUP_WIDTH
     mean = jnp.sum(jnp.dot(x, member[...], preferred_element_type=F32), axis=0, keepdims=True) / count
     centered = x.astype(F32) - to_channels(jnp.broadcast_to(mean, (8, 128)), member[...])[0:1]
@@ -176,6 +176,7 @@
     def _(step):
         stat1(step).start()
 
+    forward(0, pairs_all, (1,))
     forward(2, range(0, 2))
     all_of(st1, s1_send, s1_recv).wait_recv()
 
@@ -198,33 +199,36 @@
     mean_chan = wide[0:1]
     scale_chan = wide[1:2] * gain[...].reshape(1, CHANNELS)
     bias_chan = bias[...].reshape(1, CHANNELS)
-    normed = ((x_own[...].astype(F32) - mean_chan) * scale_chan + bias_chan).astype(BF16)
-
+
+    def normalised(block):
+        return ((block.astype(F32) - mean_chan) * scale_chan + bias_chan).astype(BF16)
+
+    own = normalised(xbuf[0])
+    nbuf[0] = own
+    for kind, load in ((0, loads[2]), (1, loads[3])):
+        load.wait()
+        fresh = jnp.dot(own, (wk, wv)[kind][...], preferred_element_type=F32).astype(BF16)
+        for pair in pairs_all:
+            kv[middle, pair, kind] = fresh[:, pair * 128 : (pair + 1) * 128]
+        result[1 + kind] = fresh
+    forward(6, range(0, 3))
     loads[1].wait()
-    query = jnp.dot(normed, wq[...], preferred_element_type=F32).astype(BF16)
-    query = query * jnp.asarray(HEAD_DIM**-0.5, BF16)
-    for pair in range(PAIRS):
-        qbuf[pair, 0] = query[:, pair * 128 : (pair + 1) * 128]
-
-    @pl.loop(0, PAIRS)
-    def _(pair):
-        @pl.loop(1, plane)
-        def _(step):
-            share(pair, step).start()
-
-    forward(6, range(0, 3))
-    loads[2].wait()
-    fresh = jnp.dot(normed, wk[...], preferred_element_type=F32).astype(BF16)
-    for pair in range(PAIRS):
-        kv[middle, pair, 0] = fresh[:, pair * 128 : (pair + 1) * 128]
-    result[1] = fresh
-    loads[3].wait()
-    fresh = jnp.dot(normed, wv[...], preferred_element_type=F32).astype(BF16)
-    for pair in range(PAIRS):
-        kv[middle, pair, 1] = fresh[:, pair * 128 : (pair + 1) * 128]
-    result[2] = fresh
+    all_of(xbuf, x_send, x_recv).wait_recv()
+
+    @pl.loop(1, plane)
+    def _(slot):
+        nbuf[slot] = normalised(xbuf[slot])
+
+    rows = plane * tokens
+    normed = nbuf[...].reshape(rows, CHANNELS)
+    for start in range(0, WIDTH, 256):
+        end = min(start + 256, WIDTH)
+        query = jnp.dot(normed, wq[:, start:end], preferred_element_type=F32).astype(BF16)
+        query = query * jnp.asarray(HEAD_DIM**-0.5, BF16)
+        for pair in range(start // 128, end // 128):
+            at = pair * 128 - start
+            qbuf[pair] = query[:, at : at + 128]
     forward(6, range(3, PAIRS))
-    need(0, half, pairs_all)
 
     lane = lax.broadcasted_iota(jnp.int32, (1, 128), 1)
     low = lane < HEAD_DIM
@@ -270,38 +274,19 @@
         now, before = jnp.exp(largest - top), jnp.exp(old_largest - top)
         return out * now + part_o[pair] * before, top, total * now + part_l[pair] * before
 
-    rows = plane * tokens
-    quarter = half // 2
-
-
+    need(0, half, pairs_all)
     attend(
-        lambda pair: qbuf[pair, 0], 1, half, range(PAIRS),
+        lambda pair: qbuf[pair, 0:tokens], 1, half, pairs_all,
         lambda pair, parts: keep(pair, 0, tokens, parts),
     )
-
-    def first_half(pairs):
-        for pair in pairs:
-            all_of(qbuf.at[pair], q_send.at[pair], q_recv.at[pair]).wait_recv()
-        attend(
-            lambda pair: qbuf[pair, 1:plane].reshape(rows - tokens, 128), 0, half, pairs,
-            lambda pair, parts: keep(pair, tokens, rows, parts),
-        )
-
-    first_half(range(0, 2))
-    first_half(range(2, PAIRS))
-    need(half, half + quarter, pairs_all)
-
-    def all_queries(pair):
-        return qbuf[pair].reshape(rows, 128)
-
     attend(
-        all_queries, half + 1, quarter, range(PAIRS),
-        lambda pair, parts: keep(pair, 0, rows, add_to(pair, parts)),
+        lambda pair: qbuf[pair, tokens:rows], 0, half, pairs_all,
+        lambda pair, parts: keep(pair, tokens, rows, parts),
     )
 
     def all_here(pair):
-        need(half + quarter, depth, [pair])
-        return all_queries(pair)
+        need(half, depth, [pair])
+        return qbuf[pair]
 
     def back(pair, slot):
         return remote(
@@ -325,7 +310,7 @@
         stats = jnp.where(within == pair, top, ostat[...])
         ostat[...] = jnp.where(within == pair + 8, total, stats)
 
-    attend(all_here, half + 1 + quarter, quarter, range(PAIRS), send_back)
+    attend(all_here, half + 1, half, pairs_all, send_back)
 
     packs = tokens // 8
     tiles = ostat[...].reshape(plane, packs, 8, 128)
@@ -349,8 +334,7 @@
     all_of(st2, s2_send, s2_recv).wait_send()
     every = kv.at[pl.ds(0, depth - 1)]
     remote(every, every, kv_send, kv_recv.at[0, 0], in_depth(1)).wait_send()
-    for pair in range(PAIRS):
-        all_of(qbuf.at[pair], q_send.at[pair], q_recv.at[pair]).wait_send()
+    all_of(xbuf, x_send, x_recv).wait_send()
 
     all_of(rstat_packed, t_send, t_recv).wait_recv()
     packed = rstat_packed[...].reshape(plane * 8, 128)
@@ -404,13 +388,14 @@
         in_specs=[anywhere, local, local] + [anywhere] * 5,
         out_specs=local,
         scratch_shapes=[
-            pltpu.VMEM((tokens, CHANNELS), BF16),
+            pltpu.VMEM((plane, tokens, CHANNELS), BF16),
             pltpu.VMEM((depth + 1, PAIRS, 2, tokens, 128), BF16),
             pltpu.VMEM((CHANNELS, WIDTH), BF16),
             pltpu.VMEM((CHANNELS, WIDTH), BF16),
             pltpu.VMEM((CHANNELS, WIDTH), BF16),
             pltpu.VMEM((CHANNELS, 128), BF16),
-            pltpu.VMEM((PAIRS, plane, tokens, 128), BF16),
+            pltpu.VMEM((plane, tokens, CHANNELS), BF16),
+            pltpu.VMEM((PAIRS, rows, 128), BF16),
             pltpu.VMEM((plane, 2, 128), F32),
             pltpu.VMEM((depth, 2, 128), F32),
             pltpu.VMEM((PAIRS, rows, 128), F32),
@@ -423,7 +408,7 @@
             pltpu.VMEM((plane, 8, 128), F32),
             dma((4,)), dma((PAIRS, 2)),
             dma, dma, dma, dma,
-            dma((PAIRS,)), dma((PAIRS,)),
+            dma, dma,
             dma, dma((depth + 1, PAIRS)),
             dma((PAIRS,)), dma((PAIRS,)),
             dma, dma,

time: 48 us -> 49.8 us (1.037)
  Pallas kernels: 46.8 us -> 48.7 us
    pallas_call x1, Pallas kernels: 46.1 us -> 48 us  [on_device(): pl.pallas_call(functools.partial(kernel, depth, plane, tokens), out_shape...]
where the time goes in v5:
time: 49.8 us; the launch traced here: 49.3 us
  Pallas kernels  48.7 us (98%)
  between operations  0.64 us (1%)
    pallas_call x1, Pallas kernels, on_device(): pl.pallas_call(functools.partial(kernel, depth, plane, tokens), out_shape...  48 us

profile of v5, /device:TPU:6, one launch (start us, length us, event | category | flops | bytes accessed | tf_op | source)
XLA Modules:
  0.0 49.3 jit_solution(10654729560647956043)
XLA Ops:
  0.6 48.0 %attention_of_plane.1.result = bf16[3,32,640]{2,1,0:T(8,128)(2,1)S(1)} custom-call(bf16[32,1280]{1,0:T(8,128)(2,1)} %x_in.1, f32[1280]{0:T(1024)} %gain.1, f32[1280]{0:T(1024)} %bias.1, bf16[1280,640]{1,0:T(8,128)(2,1)} %wq_in.1, bf16[1280,640]{1,0:T(8,128)(2,1)} %wk_in.1, bf16[1280,640]{1,0:T(8,128)(2,1)} %wv_in.1, bf16[32,640]{1,0:T(8,128)(2,1)} %k_in.1, ...), custom_call_target="tpu_custom_call" | custom-call | tf_op jit(solution)/shard_map/attention_of_plane/pallas_call | solution.py:385
  48.7 0.7 %hand_over.1 = (bf16[32,640]{1,0:T(8,128)(2,1)}, bf16[32,640]{1,0:T(8,128)(2,1)}, bf16[32,640]{1,0:T(8,128)(2,1)}) custom-call(bf16[3,32,640]{2,1,0:T(8,128)(2,1)S(1)} %attention_of_plane.1.result), custom_call_target="tpu_custom_call" | custom-call | tf_op jit(solution)/shard_map/hand_over/pallas_call | solution.py:421

commit v6 on v5

--- a/solution.py
+++ b/solution.py
@@ -15,6 +15,7 @@
 WIDTH = HEADS * HEAD_DIM
 PAIRS = HEADS // 2
 EPSILON = 1e-05
+LINE = 4
 PLANE = 8
 
 F32 = jnp.float32
@@ -52,8 +53,14 @@
     z, p = row // plane, lax.rem(row, plane)
     half = depth // 2
 
+    line = min(LINE, plane)
+
     def in_plane(step):
-        return {"rows": z * plane + lax.rem(p + step, plane)}
+        x_to = lax.rem(p // line + step // line, plane // line)
+        return {"rows": z * plane + x_to * line + lax.rem(lax.rem(p, line) + step % line, line)}
+
+    def back_in_plane(step):
+        return in_plane(step // line * line + lax.rem(line - step % line, line))
 
     def in_depth(step):
         return {"rows": lax.rem(z + step, depth) * plane + p}
@@ -103,7 +110,19 @@
         return remote(st2.at[0], st2.at[step], s2_send, s2_recv, in_depth(step))
 
     def share(step):
-        return remote(xbuf.at[0], xbuf.at[step], x_send, x_recv, in_plane(step))
+        return remote(xbuf.at[0], xbuf.at[step], x_send, x_recv.at[step, 0], in_plane(step))
+
+    def relay(side, far):
+        rows = pl.ds(side * (tokens // 2), tokens // 2)
+        near = far - 1 if side == 0 else far + 1
+        return remote(
+            xbuf.at[near, rows], xbuf.at[far, rows], x_send, x_recv.at[far, side],
+            in_plane(1 if side == 0 else line - 1),
+        )
+
+    slots = range(1, plane)
+    far_slots = [step for step in slots if line == 4 and step % line == 2]
+    near_slots = [step for step in slots if step not in far_slots]
 
     def all_of(buf, send, recv):
         rest = buf.at[pl.ds(1, buf.shape[0] - 1)]
@@ -160,7 +179,7 @@
 
     forward(0, pairs_all, (2,))
     loads[0].wait()
-    for step in range(1, plane):
+    for step in near_slots:
         share(step).start()
 
     x = xbuf[0]
@@ -189,13 +208,18 @@
         stat2(step).start()
 
     forward(2, range(2, PAIRS))
+    for step in near_slots:
+        share(step).wait_recv()
+    for far in far_slots:
+        for side in (0, 1):
+            relay(side, far).start()
     forward(4, range(0, 3))
     all_of(st2, s2_send, s2_recv).wait_recv()
 
     mean, var = merged(st2[...])
     forward(4, range(3, PAIRS))
-    line = lax.broadcasted_iota(jnp.int32, (8, 128), 0)
-    wide = to_channels(jnp.where(line == 0, mean, lax.rsqrt(var + EPSILON)), member[...])
+    sublane = lax.broadcasted_iota(jnp.int32, (8, 128), 0)
+    wide = to_channels(jnp.where(sublane == 0, mean, lax.rsqrt(var + EPSILON)), member[...])
     mean_chan = wide[0:1]
     scale_chan = wide[1:2] * gain[...].reshape(1, CHANNELS)
     bias_chan = bias[...].reshape(1, CHANNELS)
@@ -213,7 +237,9 @@
         result[1 + kind] = fresh
     forward(6, range(0, 3))
     loads[1].wait()
-    all_of(xbuf, x_send, x_recv).wait_recv()
+    for far in far_slots:
+        for side in (0, 1):
+            relay(side, far).wait_recv()
 
     @pl.loop(1, plane)
     def _(slot):
@@ -284,19 +310,26 @@
         lambda pair, parts: keep(pair, tokens, rows, parts),
     )
 
+    quarter = half // 2
+    need(half, half + quarter, pairs_all)
+    attend(
+        lambda pair: qbuf[pair], half + 1, quarter, pairs_all,
+        lambda pair, parts: keep(pair, 0, rows, add_to(pair, parts)),
+    )
+
     def all_here(pair):
-        need(half, depth, [pair])
+        need(half + quarter, depth, [pair])
         return qbuf[pair]
 
     def back(pair, slot):
         return remote(
             obuf.at[pair, slot], rbuf.at[pair, slot], o_send.at[pair], o_recv.at[pair],
-            in_plane(plane - slot),
+            back_in_plane(slot),
         )
 
     def stat_back(slot):
         return remote(
-            ostat_packed.at[slot], rstat_packed.at[slot], t_send, t_recv, in_plane(plane - slot)
+            ostat_packed.at[slot], rstat_packed.at[slot], t_send, t_recv, back_in_plane(slot)
         )
 
     ostat[...] = jnp.zeros_like(ostat)
@@ -310,7 +343,7 @@
         stats = jnp.where(within == pair, top, ostat[...])
         ostat[...] = jnp.where(within == pair + 8, total, stats)
 
-    attend(all_here, half + 1, half, pairs_all, send_back)
+    attend(all_here, half + 1 + quarter, quarter, pairs_all, send_back)
 
     packs = tokens // 8
     tiles = ostat[...].reshape(plane, packs, 8, 128)
@@ -334,7 +367,7 @@
     all_of(st2, s2_send, s2_recv).wait_send()
     every = kv.at[pl.ds(0, depth - 1)]
     remote(every, every, kv_send, kv_recv.at[0, 0], in_depth(1)).wait_send()
-    all_of(xbuf, x_send, x_recv).wait_send()
+    all_of(xbuf, x_send, x_recv.at[0, 0]).wait_send()
 
     all_of(rstat_packed, t_send, t_recv).wait_recv()
     packed = rstat_packed[...].reshape(plane * 8, 128)
@@ -408,7 +441,7 @@
             pltpu.VMEM((plane, 8, 128), F32),
             dma((4,)), dma((PAIRS, 2)),
             dma, dma, dma, dma,
-            dma, dma,
+            dma, dma((plane, 2)),
             dma, dma((depth + 1, PAIRS)),
             dma((PAIRS,)), dma((PAIRS,)),
             dma, dma,

time: 49.8 us -> 48.1 us (0.966)
  Pallas kernels: 48.7 us -> 47.2 us
    pallas_call x1, Pallas kernels: 48 us -> 46.5 us  [on_device(): pl.pallas_call(functools.partial(kernel, depth, plane, tokens), out_shape...]
where the time goes in v6:
time: 48.1 us; the launch traced here: 47.8 us
  Pallas kernels  47.2 us (98%)
  between operations  0.64 us (1%)
    pallas_call x1, Pallas kernels, on_device(): pl.pallas_call(functools.partial(kernel, depth, plane, tokens), out_shape...  46.5 us

profile of v6, /device:TPU:6, one launch (start us, length us, event | category | flops | bytes accessed | tf_op | source)
XLA Modules:
  0.0 47.8 jit_solution(5439229030552107802)
XLA Ops:
  0.6 46.5 %attention_of_plane.1.result = bf16[3,32,640]{2,1,0:T(8,128)(2,1)S(1)} custom-call(bf16[32,1280]{1,0:T(8,128)(2,1)} %x_in.1, f32[1280]{0:T(1024)} %gain.1, f32[1280]{0:T(1024)} %bias.1, bf16[1280,640]{1,0:T(8,128)(2,1)} %wq_in.1, bf16[1280,640]{1,0:T(8,128)(2,1)} %wk_in.1, bf16[1280,640]{1,0:T(8,128)(2,1)} %wv_in.1, bf16[32,640]{1,0:T(8,128)(2,1)} %k_in.1, ...), custom_call_target="tpu_custom_call" | custom-call | tf_op jit(solution)/shard_map/attention_of_plane/pallas_call | solution.py:418
  47.2 0.7 %hand_over.1 = (bf16[32,640]{1,0:T(8,128)(2,1)}, bf16[32,640]{1,0:T(8,128)(2,1)}, bf16[32,640]{1,0:T(8,128)(2,1)}) custom-call(bf16[3,32,640]{2,1,0:T(8,128)(2,1)S(1)} %attention_of_plane.1.result), custom_call_target="tpu_custom_call" | custom-call | tf_op jit(solution)/shard_map/hand_over/pallas_call | solution.py:454

commit v7 on v6

--- a/solution.py
+++ b/solution.py
@@ -16,6 +16,7 @@
 PAIRS = HEADS // 2
 EPSILON = 1e-05
 LINE = 4
+SKIPPED = 4
 PLANE = 8
 
 F32 = jnp.float32
@@ -136,7 +137,7 @@
     place = {block: at if at < middle else at + 1 for at, block in enumerate(order)}
 
     def hop(way, pair, distance):
-        before = distance - 1 if distance % 2 else distance - 2
+        before = distance - 2 if distance % 2 == 0 and distance <= SKIPPED else distance - 1
         ends = [at if way == 0 else (depth - at) % depth for at in (before, distance)]
         by = distance - before if way == 0 else depth - (distance - before)
         here, there = place[ends[0]], place[ends[1]]
@@ -164,7 +165,7 @@
     def forward(stop, pairs, hops=(2, 1)):
         if stop >= half:
             return
-        for by in hops:
+        for by in hops if stop < SKIPPED else (1,):
             for pair in pairs:
                 arrive(stop, pair)
                 for way in both_ways:
@@ -213,11 +214,10 @@
     for far in far_slots:
         for side in (0, 1):
             relay(side, far).start()
-    forward(4, range(0, 3))
+    forward(4, pairs_all)
     all_of(st2, s2_send, s2_recv).wait_recv()
 
     mean, var = merged(st2[...])
-    forward(4, range(3, PAIRS))
     sublane = lax.broadcasted_iota(jnp.int32, (8, 128), 0)
     wide = to_channels(jnp.where(sublane == 0, mean, lax.rsqrt(var + EPSILON)), member[...])
     mean_chan = wide[0:1]
@@ -229,13 +229,13 @@
 
     own = normalised(xbuf[0])
     nbuf[0] = own
+    forward(5, pairs_all)
     for kind, load in ((0, loads[2]), (1, loads[3])):
         load.wait()
         fresh = jnp.dot(own, (wk, wv)[kind][...], preferred_element_type=F32).astype(BF16)
         for pair in pairs_all:
             kv[middle, pair, kind] = fresh[:, pair * 128 : (pair + 1) * 128]
         result[1 + kind] = fresh
-    forward(6, range(0, 3))
     loads[1].wait()
     for far in far_slots:
         for side in (0, 1):
@@ -245,6 +245,7 @@
     def _(slot):
         nbuf[slot] = normalised(xbuf[slot])
 
+    forward(6, range(0, 3))
     rows = plane * tokens
     normed = nbuf[...].reshape(rows, CHANNELS)
     for start in range(0, WIDTH, 256):
@@ -305,10 +306,12 @@
         lambda pair: qbuf[pair, 0:tokens], 1, half, pairs_all,
         lambda pair, parts: keep(pair, 0, tokens, parts),
     )
-    attend(
-        lambda pair: qbuf[pair, tokens:rows], 0, half, pairs_all,
-        lambda pair, parts: keep(pair, tokens, rows, parts),
-    )
+    for pairs in (range(0, 3), range(3, PAIRS)):
+        attend(
+            lambda pair: qbuf[pair, tokens:rows], 0, half, pairs,
+            lambda pair, parts: keep(pair, tokens, rows, parts),
+        )
+        forward(7, pairs)
 
     quarter = half // 2
     need(half, half + quarter, pairs_all)
@@ -343,7 +346,8 @@
         stats = jnp.where(within == pair, top, ostat[...])
         ostat[...] = jnp.where(within == pair + 8, total, stats)
 
-    attend(all_here, half + 1 + quarter, quarter, pairs_all, send_back)
+    for pair in pairs_all:
+        attend(all_here, half + 1 + quarter, quarter, [pair], send_back)
 
     packs = tokens // 8
     tiles = ostat[...].reshape(plane, packs, 8, 128)

time: 48.1 us -> 51.6 us (1.073)
  Pallas kernels: 47.2 us -> 50.6 us
    pallas_call x1, Pallas kernels: 46.5 us -> 49.9 us  [on_device(): pl.pallas_call(functools.partial(kernel, depth, plane, tokens), out_shape...]
where the time goes in v7:
time: 51.6 us; the launch traced here: 51.2 us
  Pallas kernels  50.6 us (98%)
  between operations  0.64 us (1%)
    pallas_call x1, Pallas kernels, on_device(): pl.pallas_call(functools.partial(kernel, depth, plane, tokens), out_shape...  49.9 us

profile of v7, /device:TPU:6, one launch (start us, length us, event | category | flops | bytes accessed | tf_op | source)
XLA Modules:
  0.0 51.2 jit_solution(5080250916005731004)
XLA Ops:
  0.6 49.9 %attention_of_plane.1.result = bf16[3,32,640]{2,1,0:T(8,128)(2,1)S(1)} custom-call(bf16[32,1280]{1,0:T(8,128)(2,1)} %x_in.1, f32[1280]{0:T(1024)} %gain.1, f32[1280]{0:T(1024)} %bias.1, bf16[1280,640]{1,0:T(8,128)(2,1)} %wq_in.1, bf16[1280,640]{1,0:T(8,128)(2,1)} %wk_in.1, bf16[1280,640]{1,0:T(8,128)(2,1)} %wv_in.1, bf16[32,640]{1,0:T(8,128)(2,1)} %k_in.1, ...), custom_call_target="tpu_custom_call" | custom-call | tf_op jit(solution)/shard_map/attention_of_plane/pallas_call | solution.py:422
  50.5 0.7 %hand_over.1 = (bf16[32,640]{1,0:T(8,128)(2,1)}, bf16[32,640]{1,0:T(8,128)(2,1)}, bf16[32,640]{1,0:T(8,128)(2,1)}) custom-call(bf16[3,32,640]{2,1,0:T(8,128)(2,1)S(1)} %attention_of_plane.1.result), custom_call_target="tpu_custom_call" | custom-call | tf_op jit(solution)/shard_map/hand_over/pallas_call | solution.py:458

commit v8 on v6

--- a/solution.py
+++ b/solution.py
@@ -16,6 +16,7 @@
 PAIRS = HEADS // 2
 EPSILON = 1e-05
 LINE = 4
+BEFORE = (0, 0, 1, 0, 3, 4, 3, 6, 6)
 PLANE = 8
 
 F32 = jnp.float32
@@ -136,7 +137,7 @@
     place = {block: at if at < middle else at + 1 for at, block in enumerate(order)}
 
     def hop(way, pair, distance):
-        before = distance - 1 if distance % 2 else distance - 2
+        before = BEFORE[distance]
         ends = [at if way == 0 else (depth - at) % depth for at in (before, distance)]
         by = distance - before if way == 0 else depth - (distance - before)
         here, there = place[ends[0]], place[ends[1]]
@@ -161,15 +162,14 @@
             for distance in sorted(min(block, depth - block) for block in order[first:last]):
                 arrive(distance, pair)
 
-    def forward(stop, pairs, hops=(2, 1)):
-        if stop >= half:
-            return
-        for by in hops:
-            for pair in pairs:
-                arrive(stop, pair)
-                for way in both_ways:
-                    if stop + by <= length(way, pair):
-                        hop(way, pair, stop + by).start()
+    def forward(stop, pairs, ends=range(half, 0, -1)):
+        for distance in ends:
+            if BEFORE[distance] == stop:
+                for pair in pairs:
+                    arrive(stop, pair)
+                    for way in both_ways:
+                        if distance <= length(way, pair):
+                            hop(way, pair, distance).start()
 
     def merged(stats):
         means, spread = stats[:, 0, :], stats[:, 1, :]
@@ -177,7 +177,7 @@
         apart = means - mean
         return mean, jnp.mean(spread + apart * apart, axis=0, keepdims=True)
 
-    forward(0, pairs_all, (2,))
+    forward(0, pairs_all, (3,))
     loads[0].wait()
     for step in near_slots:
         share(step).start()
@@ -196,7 +196,7 @@
         stat1(step).start()
 
     forward(0, pairs_all, (1,))
-    forward(2, range(0, 2))
+    forward(3, range(0, 2))
     all_of(st1, s1_send, s1_recv).wait_recv()
 
     mean, var = merged(st1[...])
@@ -207,17 +207,18 @@
     def _(step):
         stat2(step).start()
 
-    forward(2, range(2, PAIRS))
+    forward(3, range(2, PAIRS))
+    forward(1, pairs_all)
     for step in near_slots:
         share(step).wait_recv()
     for far in far_slots:
         for side in (0, 1):
             relay(side, far).start()
-    forward(4, range(0, 3))
+    forward(6, range(0, 2))
     all_of(st2, s2_send, s2_recv).wait_recv()
 
     mean, var = merged(st2[...])
-    forward(4, range(3, PAIRS))
+    forward(6, range(2, PAIRS))
     sublane = lax.broadcasted_iota(jnp.int32, (8, 128), 0)
     wide = to_channels(jnp.where(sublane == 0, mean, lax.rsqrt(var + EPSILON)), member[...])
     mean_chan = wide[0:1]
@@ -235,7 +236,7 @@
         for pair in pairs_all:
             kv[middle, pair, kind] = fresh[:, pair * 128 : (pair + 1) * 128]
         result[1 + kind] = fresh
-    forward(6, range(0, 3))
+    forward(4, pairs_all)
     loads[1].wait()
     for far in far_slots:
         for side in (0, 1):
@@ -254,7 +255,6 @@
         for pair in range(start // 128, end // 128):
             at = pair * 128 - start
             qbuf[pair] = query[:, at : at + 128]
-    forward(6, range(3, PAIRS))
 
     lane = lax.broadcasted_iota(jnp.int32, (1, 128), 1)
     low = lane < HEAD_DIM

time: 48.1 us -> 51.9 us (1.079); the launches traced: 47.8 us -> 50.9 us
  Pallas kernels: 47.2 us -> 50.3 us
    pallas_call x1, Pallas kernels: 46.5 us -> 49.6 us  [on_device(): pl.pallas_call(functools.partial(kernel, depth, plane, tokens), out_shape...]
where the time goes in v8:
time: 51.9 us; the launch traced here: 50.9 us
  Pallas kernels  50.3 us (97%)
  between operations  0.64 us (1%)
    pallas_call x1, Pallas kernels, on_device(): pl.pallas_call(functools.partial(kernel, depth, plane, tokens), out_shape...  49.6 us

profile of v8, /device:TPU:6, one launch (start us, length us, event | category | flops | bytes accessed | tf_op | source)
XLA Modules:
  0.0 50.9 jit_solution(118899877352640710)
XLA Ops:
  0.6 49.6 %attention_of_plane.1.result = bf16[3,32,640]{2,1,0:T(8,128)(2,1)S(1)} custom-call(bf16[32,1280]{1,0:T(8,128)(2,1)} %x_in.1, f32[1280]{0:T(1024)} %gain.1, f32[1280]{0:T(1024)} %bias.1, bf16[1280,640]{1,0:T(8,128)(2,1)} %wq_in.1, bf16[1280,640]{1,0:T(8,128)(2,1)} %wk_in.1, bf16[1280,640]{1,0:T(8,128)(2,1)} %wv_in.1, bf16[32,640]{1,0:T(8,128)(2,1)} %k_in.1, ...), custom_call_target="tpu_custom_call" | custom-call | tf_op jit(solution)/shard_map/attention_of_plane/pallas_call | solution.py:418
  50.2 0.7 %hand_over.1 = (bf16[32,640]{1,0:T(8,128)(2,1)}, bf16[32,640]{1,0:T(8,128)(2,1)}, bf16[32,640]{1,0:T(8,128)(2,1)}) custom-call(bf16[3,32,640]{2,1,0:T(8,128)(2,1)S(1)} %attention_of_plane.1.result), custom_call_target="tpu_custom_call" | custom-call | tf_op jit(solution)/shard_map/hand_over/pallas_call | solution.py:454

commit v9 on v6

--- a/solution.py
+++ b/solution.py
@@ -343,7 +343,8 @@
         stats = jnp.where(within == pair, top, ostat[...])
         ostat[...] = jnp.where(within == pair + 8, total, stats)
 
-    attend(all_here, half + 1 + quarter, quarter, pairs_all, send_back)
+    for pair in pairs_all:
+        attend(all_here, half + 1 + quarter, quarter, [pair], send_back)
 
     packs = tokens // 8
     tiles = ostat[...].reshape(plane, packs, 8, 128)

time: 48.1 us -> 48.2 us (level)
  no operation moved by 1% of the time
where the time goes in v9:
time: 48.2 us; the launch traced here: 48 us
  Pallas kernels  47.3 us (98%)
  between operations  0.64 us (1%)
    pallas_call x1, Pallas kernels, on_device(): pl.pallas_call(functools.partial(kernel, depth, plane, tokens), out_shape...  46.7 us

profile of v9, /device:TPU:6, one launch (start us, length us, event | category | flops | bytes accessed | tf_op | source)
XLA Modules:
  0.0 48.0 jit_solution(1046165567118514898)
XLA Ops:
  0.6 46.7 %attention_of_plane.1.result = bf16[3,32,640]{2,1,0:T(8,128)(2,1)S(1)} custom-call(bf16[32,1280]{1,0:T(8,128)(2,1)} %x_in.1, f32[1280]{0:T(1024)} %gain.1, f32[1280]{0:T(1024)} %bias.1, bf16[1280,640]{1,0:T(8,128)(2,1)} %wq_in.1, bf16[1280,640]{1,0:T(8,128)(2,1)} %wk_in.1, bf16[1280,640]{1,0:T(8,128)(2,1)} %wv_in.1, bf16[32,640]{1,0:T(8,128)(2,1)} %k_in.1, ...), custom_call_target="tpu_custom_call" | custom-call | tf_op jit(solution)/shard_map/attention_of_plane/pallas_call | solution.py:419
  47.3 0.7 %hand_over.1 = (bf16[32,640]{1,0:T(8,128)(2,1)}, bf16[32,640]{1,0:T(8,128)(2,1)}, bf16[32,640]{1,0:T(8,128)(2,1)}) custom-call(bf16[3,32,640]{2,1,0:T(8,128)(2,1)S(1)} %attention_of_plane.1.result), custom_call_target="tpu_custom_call" | custom-call | tf_op jit(solution)/shard_map/hand_over/pallas_call | solution.py:455
